TPU v7x, 32 devices: a whole 2x2x4 slice. The times are simulated.
32 devices in a mesh: grp: 4 (over y, x), seq: 8 (over z, core).
Axes of the slice: x: 2, y: 2, z: 4, core: 2. Of those that a mesh axis runs over, the one named last changes fastest.
Arguments:
- block_input: bfloat16 [8192, 768], P(('grp', 'seq')), may hold values from -18 to 18
- out_grad: bfloat16 [8192, 768], P(('grp', 'seq')), may hold values from -6 to 6
- seq_span: int32 [4, 2], P('grp'), may hold values from 0 to 2048, as said below
- ln1_gain: float32 [768], replicated, may hold values from 0.5 to 1.5
- ln1_bias: float32 [768], replicated, may hold values from -2 to 2
- w_qkv: bfloat16 [768, 2304], replicated, may hold values from -0.21875 to 0.21875
- w_out: bfloat16 [768, 768], replicated, may hold values from -3 to 3
- ln2_gain: float32 [768], replicated, may hold values from 0.5 to 1.5
- ln2_bias: float32 [768], replicated, may hold values from -2 to 2
- w_up: bfloat16 [768, 3072], replicated, may hold values from -0.21875 to 0.21875
- w_down: bfloat16 [3072, 768], replicated, may hold values from -0.109375 to 0.109375
Outputs:
- block_output: bfloat16 [8192, 768], P(('grp', 'seq'))
- input_grad: bfloat16 [8192, 768], P(('grp', 'seq'))
- ln1_gain_grad: float32 [768], P(('grp', 'seq'))
- ln1_bias_grad: float32 [768], P(('grp', 'seq'))
- w_qkv_grad: float32 [768, 2304], P(('grp', 'seq'))
- w_out_grad: float32 [768, 768], P(('grp', 'seq'))
- ln2_gain_grad: float32 [768], P(('grp', 'seq'))
- ln2_bias_grad: float32 [768], P(('grp', 'seq'))
- w_up_grad: float32 [768, 3072], P(('grp', 'seq'))
- w_down_grad: float32 [3072, 768], P(('grp', 'seq'))
- rms_stats: float32 [3], replicated
Inputs may be any that keep to these rules, and one draw needn't show every extreme that they name: seq_span[g, 0] is at most 128 and seq_span[g, 1] at least 1920, so each group's sequence runs from its first device to its last.
All inputs are finite; a program needn't handle non-finite values.
Results may differ from a plain program's by a relative error of at most 0.012.
Values may be sent and summed in bfloat16 or wider, within the bound.
A program may use at most 128 MiB of HBM per device.

v0:
```python
import jax
import jax.numpy as jnp
from jax import lax
from jax.sharding import PartitionSpec as P

D = 768
HEADS = 12
HEAD_DIM = 64


epsilon = 1e-05


def passed_along(array, axis, by):
    devices = lax.axis_size(axis)
    pairs = [(i, i + by) for i in range(devices) if 0 <= i + by < devices]
    return lax.ppermute(array, axis, pairs)


def shifted(array, axis, by):
    devices = lax.axis_size(axis)
    return lax.ppermute(array, axis, [(i, (i + by) % devices) for i in range(devices)])


def layer_norm(vector, scale_vec, shift_vec):
    row_mean = jnp.mean(vector, axis=-1, keepdims=True)
    centered = vector - row_mean
    variance = jnp.mean(centered * centered, axis=-1, keepdims=True)
    return centered * lax.rsqrt(variance + epsilon) * scale_vec + shift_vec


def contract_rows(left, right):
    return lax.dot_general(
        left, right, (((0,), (0,)), ((), ())), preferred_element_type=jnp.float32
    )


def contract_cols(left, right):
    return lax.dot_general(
        left, right, (((1,), (1,)), ((), ())), preferred_element_type=jnp.float32
    )


def score_terms(queries, key_block, query_pos, key_pos, seq_first, seq_limit):
    scores = (
        jnp.einsum("qhd,khd->qhk", queries, key_block, preferred_element_type=jnp.float32) * 0.125
    )
    query_valid = (query_pos >= seq_first) & (query_pos < seq_limit)
    key_valid = (key_pos >= seq_first) & (key_pos < seq_limit)
    allowed = (key_pos[None, :] <= query_pos[:, None]) & (
        query_valid[:, None] & key_valid[None, :] | (key_pos[None, :] == query_pos[:, None])
    )
    magnitude = jnp.sqrt(scores * scores + 1.0)
    signed_part = scores / magnitude
    exp_terms = jnp.where(allowed[:, None, :], jnp.exp(magnitude), 0.0)
    return (magnitude, signed_part, exp_terms)


def split_pair(kv_pair):
    count_rows = kv_pair.shape[0]
    key_block = kv_pair[:, :D].reshape(count_rows, HEADS, HEAD_DIM)
    value_block = kv_pair[:, D:].reshape(count_rows, HEADS, HEAD_DIM)
    return (key_block, value_block)


def forward_block(running, kv_pair, key_start, queries, query_pos, seq_first, seq_limit):
    totals, unnorm = running
    key_block, value_block = split_pair(kv_pair)
    key_pos = key_start + jnp.arange(kv_pair.shape[0], dtype=jnp.int32)
    magnitude, signed_part, exp_terms = score_terms(
        queries, key_block, query_pos, key_pos, seq_first, seq_limit
    )
    weights = (signed_part * exp_terms).astype(jnp.bfloat16)
    totals = totals + jnp.sum(exp_terms, axis=-1)
    unnorm = unnorm + jnp.einsum(
        "qhk,khd->qhd", weights, value_block, preferred_element_type=jnp.float32
    )
    return (totals, unnorm)


def grad_core(
    kv_pair, key_start, queries, query_pos, seq_first, seq_limit, grad_unnorm, grad_totals
):
    key_block, value_block = split_pair(kv_pair)
    key_pos = key_start + jnp.arange(kv_pair.shape[0], dtype=jnp.int32)
    magnitude, signed_part, exp_terms = score_terms(
        queries, key_block, query_pos, key_pos, seq_first, seq_limit
    )
    weights = (signed_part * exp_terms).astype(jnp.bfloat16)
    grad_weights = jnp.einsum(
        "qhd,khd->qhk", grad_unnorm, value_block, preferred_element_type=jnp.float32
    )
    grad_scores = (
        grad_weights * exp_terms / (magnitude * magnitude * magnitude)
        + (grad_weights * signed_part + grad_totals[:, :, None]) * exp_terms * signed_part
    )
    return (key_block, weights, grad_scores.astype(jnp.bfloat16))


def backward_block(
    kv_pair, key_start, queries, query_pos, seq_first, seq_limit, grad_unnorm, grad_totals
):
    key_block, weights, grad_scores = grad_core(
        kv_pair, key_start, queries, query_pos, seq_first, seq_limit, grad_unnorm, grad_totals
    )
    count_rows = kv_pair.shape[0]
    grad_query = (
        jnp.einsum("qhk,khd->qhd", grad_scores, key_block, preferred_element_type=jnp.float32)
        * 0.125
    )
    grad_key = (
        jnp.einsum("qhk,qhd->khd", grad_scores, queries, preferred_element_type=jnp.float32) * 0.125
    )
    grad_value = jnp.einsum(
        "qhk,qhd->khd", weights, grad_unnorm, preferred_element_type=jnp.float32
    )
    grad_pair = jnp.concatenate(
        [grad_key.reshape(count_rows, D), grad_value.reshape(count_rows, D)], axis=1
    )
    return (grad_query, grad_pair)


def per_device(
    block_input,
    out_grad,
    seq_span,
    ln1_gain,
    ln1_bias,
    w_qkv,
    w_out,
    ln2_gain,
    ln2_bias,
    w_up,
    w_down,
):
    tok_rows = block_input.shape[0]
    feat_width = block_input.shape[1]
    seq_count = lax.axis_size("seq")
    seq_index = lax.axis_index("seq")
    query_pos = seq_index * tok_rows + jnp.arange(tok_rows, dtype=jnp.int32)
    query_last = query_pos[tok_rows - 1]
    seq_first = seq_span[0, 0]
    seq_limit = seq_span[0, 1]
    inputs = block_input.astype(jnp.float32)
    normed = layer_norm(inputs, ln1_gain, ln1_bias).astype(jnp.bfloat16)
    proj_qkv = jnp.dot(normed, w_qkv, preferred_element_type=jnp.float32).astype(jnp.bfloat16)
    queries = proj_qkv[:, :feat_width].reshape(tok_rows, HEADS, HEAD_DIM)
    kv_pair = proj_qkv[:, feat_width:]

    def visit_block(running, shard_rows, key_start):
        return lax.cond(
            key_start <= query_last,
            lambda state_in: forward_block(
                state_in, shard_rows, key_start, queries, query_pos, seq_first, seq_limit
            ),
            lambda state_in: state_in,
            running,
        )

    empty = (
        jnp.zeros((tok_rows, HEADS), jnp.float32),
        jnp.zeros((tok_rows, HEADS, HEAD_DIM), jnp.float32),
    )
    first_state = visit_block(empty, kv_pair, seq_index * tok_rows)

    def forward_hop(hop_count, loop_state):
        moving, running = loop_state
        moving = passed_along(moving, "seq", 1)
        source = (seq_index - hop_count) % seq_count
        return (moving, visit_block(running, moving, source * tok_rows))

    _, (totals, unnorm) = lax.fori_loop(1, seq_count, forward_hop, (kv_pair, first_state))
    mixed_heads = (unnorm / totals[:, :, None]).reshape(tok_rows, feat_width).astype(jnp.bfloat16)
    attn_out = jnp.dot(mixed_heads, w_out, preferred_element_type=jnp.float32)
    middle = inputs + attn_out
    normed_two = layer_norm(middle, ln2_gain, ln2_bias).astype(jnp.bfloat16)
    up_proj = jnp.dot(normed_two, w_up, preferred_element_type=jnp.float32)
    activated = jax.nn.gelu(up_proj, approximate=True).astype(jnp.bfloat16)
    mlp_out = jnp.dot(activated, w_down, preferred_element_type=jnp.float32)
    output = middle + mlp_out
    valid_rows = ((query_pos >= seq_first) & (query_pos < seq_limit)).astype(jnp.float32)[:, None]
    rms_parts = lax.psum(
        (
            jnp.sum(valid_rows * output * output),
            jnp.sum(valid_rows * attn_out * attn_out),
            jnp.sum(valid_rows * mlp_out * mlp_out),
            jnp.sum(valid_rows) * feat_width,
        ),
        ("grp", "seq"),
    )
    rms_stats = jnp.sqrt(jnp.stack([rms_parts[0], rms_parts[1], rms_parts[2]]) / rms_parts[3])
    grad_w_down = contract_rows(activated, out_grad)
    grad_activated = contract_cols(out_grad, w_down)
    _, gelu_pull = jax.vjp(lambda pre_act: jax.nn.gelu(pre_act, approximate=True), up_proj)
    grad_up = gelu_pull(grad_activated)[0].astype(jnp.bfloat16)
    grad_w_up = contract_rows(normed_two, grad_up)
    grad_norm_two = contract_cols(grad_up, w_up)
    _, norm_pull_two = jax.vjp(layer_norm, middle, ln2_gain, ln2_bias)
    grad_mid_norm, grad_gain_two, grad_bias_two = norm_pull_two(grad_norm_two)
    grad_middle = out_grad.astype(jnp.float32) + grad_mid_norm
    grad_attn = grad_middle.astype(jnp.bfloat16)
    grad_w_out = contract_rows(mixed_heads, grad_attn)
    grad_mixed = contract_cols(grad_attn, w_out).reshape(tok_rows, HEADS, HEAD_DIM)
    grad_unnorm = (grad_mixed / totals[:, :, None]).astype(jnp.bfloat16)
    grad_totals = -jnp.sum(grad_mixed * unnorm, axis=-1) / (totals * totals)

    def back_block(grad_run, shard_rows, key_start):

        def compute_block(grad_in):
            grad_query, grad_pair = backward_block(
                shard_rows,
                key_start,
                queries,
                query_pos,
                seq_first,
                seq_limit,
                grad_unnorm,
                grad_totals,
            )
            return (grad_in + grad_query, grad_pair)

        def skip_block(grad_in):
            return (grad_in, jnp.zeros((shard_rows.shape[0], 2 * feat_width), jnp.float32))

        return lax.cond(key_start <= query_last, compute_block, skip_block, grad_run)

    grad_start = jnp.zeros((tok_rows, HEADS, HEAD_DIM), jnp.float32)
    grad_queries, local_terms = back_block(grad_start, kv_pair, seq_index * tok_rows)

    def backward_hop(hop_count, loop_state):
        moving, grad_acc, grad_run = loop_state
        moving = passed_along(moving, "seq", 1)
        grad_acc = shifted(grad_acc.astype(jnp.bfloat16), "seq", 1).astype(grad_acc.dtype)
        source = (seq_index - hop_count) % seq_count
        grad_run, new_terms = back_block(grad_run, moving, source * tok_rows)
        return (moving, grad_acc + new_terms, grad_run)

    _, grad_acc, grad_queries = lax.fori_loop(
        1, seq_count, backward_hop, (kv_pair, local_terms, grad_queries)
    )
    grad_kv = shifted(grad_acc.astype(jnp.bfloat16), "seq", 1).astype(grad_acc.dtype)
    grad_qkv = jnp.concatenate(
        [grad_queries.reshape(tok_rows, feat_width), grad_kv], axis=1
    ).astype(jnp.bfloat16)
    grad_w_qkv = contract_rows(normed, grad_qkv)
    grad_norm_one = contract_cols(grad_qkv, w_qkv)
    _, norm_pull_one = jax.vjp(layer_norm, inputs, ln1_gain, ln1_bias)
    grad_in_norm, grad_gain_one, grad_bias_one = norm_pull_one(grad_norm_one)
    input_grad = (grad_middle + grad_in_norm).astype(jnp.bfloat16)
    summed = (
        lax.psum_scatter(grad_gain_one, ("grp", "seq"), scatter_dimension=0, tiled=True),
        lax.psum_scatter(grad_bias_one, ("grp", "seq"), scatter_dimension=0, tiled=True),
        lax.psum_scatter(grad_w_qkv, ("grp", "seq"), scatter_dimension=0, tiled=True),
        lax.psum_scatter(grad_w_out, ("grp", "seq"), scatter_dimension=0, tiled=True),
        lax.psum_scatter(grad_gain_two, ("grp", "seq"), scatter_dimension=0, tiled=True),
        lax.psum_scatter(grad_bias_two, ("grp", "seq"), scatter_dimension=0, tiled=True),
        lax.psum_scatter(grad_w_up, ("grp", "seq"), scatter_dimension=0, tiled=True),
        lax.psum_scatter(grad_w_down, ("grp", "seq"), scatter_dimension=0, tiled=True),
    )
    return (
        output.astype(jnp.bfloat16),
        input_grad,
        summed[0],
        summed[1],
        summed[2],
        summed[3],
        summed[4],
        summed[5],
        summed[6],
        summed[7],
        rms_stats,
    )


def solution(mesh):
    placed = (
        P(("grp", "seq"), None),
        P(("grp", "seq"), None),
        P("grp", None),
        P(),
        P(),
        P(),
        P(),
        P(),
        P(),
        P(),
        P(),
    )
    return jax.shard_map(
        per_device,
        mesh=mesh,
        in_specs=placed,
        out_specs=(
            P(("grp", "seq"), None),
            P(("grp", "seq"), None),
            P(("grp", "seq")),
            P(("grp", "seq")),
            P(("grp", "seq"), None),
            P(("grp", "seq"), None),
            P(("grp", "seq")),
            P(("grp", "seq")),
            P(("grp", "seq"), None),
            P(("grp", "seq"), None),
            P(),
        ),
        check_vma=False,
    )
```

profile of v0, /device:TPU:0, one launch (start us, length us, event | category | flops | bytes accessed | tf_op | source)
XLA Modules:
  0.0 902.4 jit_solution(755135347390046226)
XLA Ops:
  10.4 2.2 convolution_convert_fusion
  15.0 2.3 copy.66
  17.2 2.1 copy.92
  23.1 13.1 %conditional.4 = (f32[256,12]{0,1:T(8,128)S(1)}, f32[256,12,64]{0,2,1:T(8,128)}) conditional(s32[]{:T(128)} %convert_element_type.117, () %tuple.90, (s32[]{:T(128)}, s32[256]{0:T(256)}, s32[]{:T(128)}, s32[]{:T(128)}, bf16[256,1536]{1,0:T(8,128)(2,1)}, /*index=5*/bf16[256,12,64]{0,2,1:T(8,128)(2,1)}) %tuple.198), branch_computations={%region_2.0_spmd, %region_3.5_spmd} | conditional | flops 211090432 | bytes 11879484 | solution.py:151
  26.6 2.3 copy.65
  30.1 3.0 fusion.10
  33.1 3.0 fusion.13
  36.3 126.1 %while.43 = (s32[]{:T(128)}, bf16[256,1536]{0,1:T(8,128)(2,1)}, f32[256,12]{0,1:T(8,128)S(1)}, f32[256,12,64]{0,2,1:T(8,128)}, s32[]{:T(128)}, /*index=5*/s32[]{...) while((s32[]{:T(128)}, bf16[256,1536]{0,1:T(8,128)(2,1)}, ...), condition=%wide.region_9.10_spmd.clone, body=%wide.region_5.9_spmd.clone.sunk | while | flops 211290384 | bytes 15588812 | solution.py:172
  36.3 3.3 collective-permute-start
  41.4 2.1 copy.100
  43.5 23.0 %collective-permute-start = (bf16[256,1536]{0,1:T(8,128)(2,1)}, bf16[256,1536]{0,1:T(8,128)(2,1)}, u32[]{:S(2)}, u32[]{:S(2)}) collective-permute-start(bf16[256,1536]{0,1:T(8,128)(2,1)} %get-tuple-element.1112), channel_id=1, source_target_pairs={{0,1},{1,2},{2,3},{3,4},{4,5},{5,6},{6,7},{8,9},{9,10},{10,11},{11... | collective-permute-start | bytes 2359304 | tf_op jit(solution)/shard_map/while/body/eval_jaxpr/ppermute | solution.py:17
  68.4 2.1 copy.100
  70.4 12.3 %collective-permute-start = (bf16[256,1536]{0,1:T(8,128)(2,1)}, bf16[256,1536]{0,1:T(8,128)(2,1)}, u32[]{:S(2)}, u32[]{:S(2)}) collective-permute-start(bf16[256,1536]{0,1:T(8,128)(2,1)} %get-tuple-element.1112), channel_id=1, source_target_pairs={{0,1},{1,2},{2,3},{3,4},{4,5},{5,6},{6,7},{8,9},{9,10},{10,11},{11... | collective-permute-start | bytes 2359304 | tf_op jit(solution)/shard_map/while/body/eval_jaxpr/ppermute | solution.py:17
  86.7 22.8 %collective-permute-start = (bf16[256,1536]{0,1:T(8,128)(2,1)}, bf16[256,1536]{0,1:T(8,128)(2,1)}, u32[]{:S(2)}, u32[]{:S(2)}) collective-permute-start(bf16[256,1536]{0,1:T(8,128)(2,1)} %get-tuple-element.1112), channel_id=1, source_target_pairs={{0,1},{1,2},{2,3},{3,4},{4,5},{5,6},{6,7},{8,9},{9,10},{10,11},{11... | collective-permute-start | bytes 2359304 | tf_op jit(solution)/shard_map/while/body/eval_jaxpr/ppermute | solution.py:17
  113.4 12.3 %collective-permute-start = (bf16[256,1536]{0,1:T(8,128)(2,1)}, bf16[256,1536]{0,1:T(8,128)(2,1)}, u32[]{:S(2)}, u32[]{:S(2)}) collective-permute-start(bf16[256,1536]{0,1:T(8,128)(2,1)} %get-tuple-element.1112), channel_id=1, source_target_pairs={{0,1},{1,2},{2,3},{3,4},{4,5},{5,6},{6,7},{8,9},{9,10},{10,11},{11... | collective-permute-start | bytes 2359304 | tf_op jit(solution)/shard_map/while/body/eval_jaxpr/ppermute | solution.py:17
  129.6 12.5 %collective-permute-start = (bf16[256,1536]{0,1:T(8,128)(2,1)}, bf16[256,1536]{0,1:T(8,128)(2,1)}, u32[]{:S(2)}, u32[]{:S(2)}) collective-permute-start(bf16[256,1536]{0,1:T(8,128)(2,1)} %get-tuple-element.1112), channel_id=1, source_target_pairs={{0,1},{1,2},{2,3},{3,4},{4,5},{5,6},{6,7},{8,9},{9,10},{10,11},{11... | collective-permute-start | bytes 2359304 | tf_op jit(solution)/shard_map/while/body/eval_jaxpr/ppermute | solution.py:17
  146.1 12.3 %collective-permute-start = (bf16[256,1536]{0,1:T(8,128)(2,1)}, bf16[256,1536]{0,1:T(8,128)(2,1)}, u32[]{:S(2)}, u32[]{:S(2)}) collective-permute-start(bf16[256,1536]{0,1:T(8,128)(2,1)} %get-tuple-element.1112), channel_id=1, source_target_pairs={{0,1},{1,2},{2,3},{3,4},{4,5},{5,6},{6,7},{8,9},{9,10},{10,11},{11... | collective-permute-start | bytes 2359304 | tf_op jit(solution)/shard_map/while/body/eval_jaxpr/ppermute | solution.py:17
  167.7 3.9 fusion.121
  171.7 5.1 fusion.80
  178.9 3.7 fusion.92
  191.3 15.2 %conditional.5 = (f32[256,12,64]{0,2,1:T(8,128)}, bf16[256,1536]{0,1:T(8,128)(2,1)}) conditional(s32[]{:T(128)} %convert_element_type.117, () %tuple.93, (bf16[256,1536]{1,0:T(8,128)(2,1)}, bf16[256,12,64]{0,2,1:T(8,128)(2,1)}, s32[]{:T(128)}, s32[256]{0:T(256)}, s32[]{:T(128)}, /*index=5*/s32[]{:T(128)}, bf16[256,12,64]{0,2,1:T(8,128)(2,1)}, ...), branch_computations={%region_15.16_spmd, %region_16.17_spmd} | conditional | flops 523110400 | bytes 26612880 | solution.py:225
  191.5 2.3 copy.68
  198.1 3.2 fusion.48
  202.6 2.2 fusion.49
  206.6 249.9 %while.44 = (s32[]{:T(128)}, bf16[256,1536]{0,1:T(8,128)(2,1)}, bf16[256,1536]{0,1:T(8,128)(2,1)}, f32[256,12,64]{0,2,1:T(8,128)}, s32[]{:T(128)}, /*index=5*/s3...) while((s32[]{:T(128)}, bf16[256,1536]{0,1:T(8,128)(2,1)}, ...), condition=%wide.region_20.21_spmd.clone, body=%wide.region_17.20_spmd.clone.sunk | while | flops 523110656 | bytes 39194184 | solution.py:238
  206.6 22.8 %collective-permute-start.1 = (bf16[256,1536]{0,1:T(8,128)(2,1)}, bf16[256,1536]{0,1:T(8,128)(2,1)}, u32[]{:S(2)}, u32[]{:S(2)}) collective-permute-start(bf16[256,1536]{0,1:T(8,128)(2,1)} %get-tuple-element.1163), channel_id=1, source_target_pairs={{0,1},{1,2},{2,3},{3,4},{4,5},{5,6},{6,7},{8,9},{9,10},{10,11},{11... | collective-permute-start | bytes 2359304 | tf_op jit(solution)/shard_map/while/body/eval_jaxpr/ppermute | solution.py:17
  231.9 2.1 copy.116
  233.9 40.7 %collective-permute-done.2 = bf16[256,1536]{0,1:T(8,128)(2,1)} collective-permute-done((bf16[256,1536]{0,1:T(8,128)(2,1)}, bf16[256,1536]{0,1:T(8,128)(2,1)}, u32[]{:S(2)}, u32[]{:S(2)}) %collective-permute-start.2) | collective-permute-done | bytes 786464 | tf_op jit(solution)/shard_map/while/body/eval_jaxpr/ppermute | solution.py:22
  274.6 2.3 convert_add_fusion.4
  276.9 2.2 collective-permute-start.1
  280.5 2.1 copy.116
  282.6 16.5 %collective-permute-done.2 = bf16[256,1536]{0,1:T(8,128)(2,1)} collective-permute-done((bf16[256,1536]{0,1:T(8,128)(2,1)}, bf16[256,1536]{0,1:T(8,128)(2,1)}, u32[]{:S(2)}, u32[]{:S(2)}) %collective-permute-start.2) | collective-permute-done | bytes 786464 | tf_op jit(solution)/shard_map/while/body/eval_jaxpr/ppermute | solution.py:22
  299.1 2.3 convert_add_fusion.4
  301.3 2.2 collective-permute-start.1
  306.3 2.1 copy.116
  308.4 19.4 %collective-permute-done.2 = bf16[256,1536]{0,1:T(8,128)(2,1)} collective-permute-done((bf16[256,1536]{0,1:T(8,128)(2,1)}, bf16[256,1536]{0,1:T(8,128)(2,1)}, u32[]{:S(2)}, u32[]{:S(2)}) %collective-permute-start.2) | collective-permute-done | bytes 786464 | tf_op jit(solution)/shard_map/while/body/eval_jaxpr/ppermute | solution.py:22
  327.7 2.3 convert_add_fusion.4
  330.0 2.2 collective-permute-start.1
  334.4 2.1 copy.116
  336.5 24.0 %collective-permute-done.2 = bf16[256,1536]{0,1:T(8,128)(2,1)} collective-permute-done((bf16[256,1536]{0,1:T(8,128)(2,1)}, bf16[256,1536]{0,1:T(8,128)(2,1)}, u32[]{:S(2)}, u32[]{:S(2)}) %collective-permute-start.2) | collective-permute-done | bytes 786464 | tf_op jit(solution)/shard_map/while/body/eval_jaxpr/ppermute | solution.py:22
  360.5 2.3 convert_add_fusion.4
  362.8 2.2 collective-permute-start.1
  366.4 2.1 copy.116
  368.5 24.2 %collective-permute-done.2 = bf16[256,1536]{0,1:T(8,128)(2,1)} collective-permute-done((bf16[256,1536]{0,1:T(8,128)(2,1)}, bf16[256,1536]{0,1:T(8,128)(2,1)}, u32[]{:S(2)}, u32[]{:S(2)}) %collective-permute-start.2) | collective-permute-done | bytes 786464 | tf_op jit(solution)/shard_map/while/body/eval_jaxpr/ppermute | solution.py:22
  392.7 2.3 convert_add_fusion.4
  395.0 2.2 collective-permute-start.1
  398.6 2.1 copy.116
  400.7 22.8 %collective-permute-done.2 = bf16[256,1536]{0,1:T(8,128)(2,1)} collective-permute-done((bf16[256,1536]{0,1:T(8,128)(2,1)}, bf16[256,1536]{0,1:T(8,128)(2,1)}, u32[]{:S(2)}, u32[]{:S(2)}) %collective-permute-start.2) | collective-permute-done | bytes 786464 | tf_op jit(solution)/shard_map/while/body/eval_jaxpr/ppermute | solution.py:22
  423.5 2.3 convert_add_fusion.4
  425.7 2.2 collective-permute-start.1
  429.4 2.1 copy.116
  431.5 22.8 %collective-permute-done.2 = bf16[256,1536]{0,1:T(8,128)(2,1)} collective-permute-done((bf16[256,1536]{0,1:T(8,128)(2,1)}, bf16[256,1536]{0,1:T(8,128)(2,1)}, u32[]{:S(2)}, u32[]{:S(2)}) %collective-permute-start.2) | collective-permute-done | bytes 786464 | tf_op jit(solution)/shard_map/while/body/eval_jaxpr/ppermute | solution.py:22
  454.2 2.3 convert_add_fusion.4
  457.7 25.8 %collective-permute-done.3 = bf16[256,1536]{0,1:T(8,128)(2,1)S(1)} collective-permute-done((bf16[256,1536]{0,1:T(8,128)(2,1)}, bf16[256,1536]{0,1:T(8,128)(2,1)S(1)}, u32[]{:S(2)}, u32[]{:S(2)}) %collective-permute-start.3) | collective-permute-done | bytes 786464 | tf_op jit(solution)/shard_map/ppermute | solution.py:22
  484.4 5.2 fusion.95
  490.4 6.9 fusion.106
  497.6 7.9 fusion.108
  506.2 3.3 fusion.110
  510.6 42.0 %all-reduce.4 = (f32[768]{0:T(1024)}, f32[768]{0:T(1024)}, f32[768]{0:T(1024)}, f32[768]{0:T(1024)}, f32[1]{0:T(128)}, /*index=5*/f32[1]{0:T(128)}, f32[1]{0:T(128)}, f32[]{:T(128)}) all-reduce(f32[768]{0:T(1024)S(1)} %get-tuple-element.842, f32[768]{0:T(1024)} %get-tuple-element.849, ...), channel_id=2, replica_groups=mesh['grp'=4,'seq'=8] {'grp','seq'}, use_global_device_ids=true, to_apply=%region_24.25.clone | all-reduce | flops 3076 | bytes 24608
  557.6 3.0 fusion.100
  561.3 2.9 add_convert_fusion
  564.2 47.8 %reduce-scatter.5.cloned.1.call-done = f32[24,2304]{1,0:T(8,128)} async-done(((f32[768,2304]{1,0:T(8,128)}), f32[24,2304]{1,0:T(8,128)}) %reduce-scatter.5.cloned.1.call-update) | async-done | bytes 221200 | tf_op jit(solution)/shard_map/reduce_scatter | solution.py:253
  612.0 141.4 %reduce-scatter.9.cloned.1.call-done = f32[24,3072]{1,0:T(8,128)} async-done(((f32[768,3072]{1,0:T(8,128)}), f32[24,3072]{1,0:T(8,128)}) %reduce-scatter.9.cloned.1.call-update) | async-done | bytes 294928 | tf_op jit(solution)/shard_map/reduce_scatter | solution.py:257
  753.4 141.9 %reduce-scatter.11.cloned.1.call-done = f32[96,768]{1,0:T(8,128)} async-done(((f32[3072,768]{1,0:T(8,128)}), f32[96,768]{1,0:T(8,128)}) %reduce-scatter.11.cloned.1.call-update) | async-done | bytes 294928 | tf_op jit(solution)/shard_map/reduce_scatter | solution.py:258
  (193 shorter events, 74.4 us)
Async XLA Ops:
  7.2 3.2 copy-start
  7.2 557.0 %reduce-scatter.7.cloned.1.call-start = ((), (), s32[]{:S(2)}) async-start(), calls=%async_computation.5 | async-start | bytes 2433024 | tf_op jit(solution)/shard_map/reduce_scatter | solution.py:254
  8.5 4.1 copy-start.22
  9.8 0.6 copy-start.34
  10.4 2.2 copy-start.24
  10.4 4.0 copy-start.36
  19.3 0.6 copy-start.27
  30.0 3.0 copy-start.21
  36.3 4.6 collective-permute-start
  43.5 24.3 %collective-permute-start = (bf16[256,1536]{0,1:T(8,128)(2,1)}, bf16[256,1536]{0,1:T(8,128)(2,1)}, u32[]{:S(2)}, u32[]{:S(2)}) collective-permute-start(bf16[256,1536]{0,1:T(8,128)(2,1)} %get-tuple-element.1112), channel_id=1, source_target_pairs={{0,1},{1,2},{2,3},{3,4},{4,5},{5,6},{6,7},{8,9},{9,10},{10,11},{11... | collective-permute-start | bytes 2359304 | tf_op jit(solution)/shard_map/while/body/eval_jaxpr/ppermute | solution.py:17
  70.4 13.6 %collective-permute-start = (bf16[256,1536]{0,1:T(8,128)(2,1)}, bf16[256,1536]{0,1:T(8,128)(2,1)}, u32[]{:S(2)}, u32[]{:S(2)}) collective-permute-start(bf16[256,1536]{0,1:T(8,128)(2,1)} %get-tuple-element.1112), channel_id=1, source_target_pairs={{0,1},{1,2},{2,3},{3,4},{4,5},{5,6},{6,7},{8,9},{9,10},{10,11},{11... | collective-permute-start | bytes 2359304 | tf_op jit(solution)/shard_map/while/body/eval_jaxpr/ppermute | solution.py:17
  86.7 24.1 %collective-permute-start = (bf16[256,1536]{0,1:T(8,128)(2,1)}, bf16[256,1536]{0,1:T(8,128)(2,1)}, u32[]{:S(2)}, u32[]{:S(2)}) collective-permute-start(bf16[256,1536]{0,1:T(8,128)(2,1)} %get-tuple-element.1112), channel_id=1, source_target_pairs={{0,1},{1,2},{2,3},{3,4},{4,5},{5,6},{6,7},{8,9},{9,10},{10,11},{11... | collective-permute-start | bytes 2359304 | tf_op jit(solution)/shard_map/while/body/eval_jaxpr/ppermute | solution.py:17
  113.4 13.6 %collective-permute-start = (bf16[256,1536]{0,1:T(8,128)(2,1)}, bf16[256,1536]{0,1:T(8,128)(2,1)}, u32[]{:S(2)}, u32[]{:S(2)}) collective-permute-start(bf16[256,1536]{0,1:T(8,128)(2,1)} %get-tuple-element.1112), channel_id=1, source_target_pairs={{0,1},{1,2},{2,3},{3,4},{4,5},{5,6},{6,7},{8,9},{9,10},{10,11},{11... | collective-permute-start | bytes 2359304 | tf_op jit(solution)/shard_map/while/body/eval_jaxpr/ppermute | solution.py:17
  129.6 13.8 %collective-permute-start = (bf16[256,1536]{0,1:T(8,128)(2,1)}, bf16[256,1536]{0,1:T(8,128)(2,1)}, u32[]{:S(2)}, u32[]{:S(2)}) collective-permute-start(bf16[256,1536]{0,1:T(8,128)(2,1)} %get-tuple-element.1112), channel_id=1, source_target_pairs={{0,1},{1,2},{2,3},{3,4},{4,5},{5,6},{6,7},{8,9},{9,10},{10,11},{11... | collective-permute-start | bytes 2359304 | tf_op jit(solution)/shard_map/while/body/eval_jaxpr/ppermute | solution.py:17
  146.1 13.6 %collective-permute-start = (bf16[256,1536]{0,1:T(8,128)(2,1)}, bf16[256,1536]{0,1:T(8,128)(2,1)}, u32[]{:S(2)}, u32[]{:S(2)}) collective-permute-start(bf16[256,1536]{0,1:T(8,128)(2,1)} %get-tuple-element.1112), channel_id=1, source_target_pairs={{0,1},{1,2},{2,3},{3,4},{4,5},{5,6},{6,7},{8,9},{9,10},{10,11},{11... | collective-permute-start | bytes 2359304 | tf_op jit(solution)/shard_map/while/body/eval_jaxpr/ppermute | solution.py:17
  162.3 5.4 copy-start.6
  165.5 17.1 %copy-start.4 = (f32[256,768]{1,0:T(8,128)}, f32[256,768]{1,0:T(8,128)S(1)}, u32[]{:S(2)}) copy-start(f32[256,768]{1,0:T(8,128)S(1)} %get-tuple-element.913) | copy-start | bytes 2359300
  165.5 17.0 %copy-start.26 = (f32[256]{0:T(256)}, f32[256]{0:T(256)S(1)}, u32[]{:S(2)}) copy-start(f32[256]{0:T(256)S(1)} %broadcast_multiply_fusion) | copy-start | bytes 3076
  167.7 14.9 %copy-start.31 = (f32[256]{0:T(256)}, f32[256]{0:T(256)S(1)}, u32[]{:S(2)}) copy-start(f32[256]{0:T(256)S(1)} %get-tuple-element.941) | copy-start | bytes 3076
  167.7 3.9 copy-start.16
  167.7 4.0 copy-start.19
  167.7 9.1 %slice-start.2 = ((s8[4718592]{0:T(1024)(128)(4,1)}), s8[4194304]{0:T(1024)(128)(4,1)S(1)}, s32[]{:S(2)}) async-start(s8[4718592]{0:T(1024)(128)(4,1)} %bitcast.241), calls=%async_computation.10 | async-start | bytes 8388608
  167.7 11.2 %slice-start = ((s8[4718592]{0:T(1024)(128)(4,1)}), s8[4194304]{0:T(1024)(128)(4,1)S(1)}, s32[]{:S(2)}) async-start(s8[4718592]{0:T(1024)(128)(4,1)} %bitcast.227), calls=%async_computation.8 | async-start | bytes 8388608
  171.7 5.1 slice-start.3
  171.7 7.2 slice-start.1
  176.8 1.5 copy-start.10
  176.8 2.1 copy-start.7
  182.9 0.9 copy-start.5
  183.0 1.1 copy-start.33
  184.0 0.7 copy-start.8
  186.7 425.3 %reduce-scatter.5.cloned.1.call-start = ((), (), s32[]{:S(2)}) async-start(), calls=%async_computation.4 | async-start | bytes 7299072 | tf_op jit(solution)/shard_map/reduce_scatter | solution.py:253
  193.8 2.9 copy-start.28
  193.8 4.3 copy-start.13
  193.8 4.3 copy-start.29
  202.6 2.2 copy-start.1
  206.5 277.9 %copy-start.15 = (f32[768]{0:T(1024)S(1)}, f32[768]{0:T(1024)}, u32[]{:S(2)}) copy-start(f32[768]{0:T(1024)} %param.26) | copy-start | bytes 9220
  206.5 277.9 %copy-start.18 = (f32[768]{0:T(1024)S(1)}, f32[768]{0:T(1024)}, u32[]{:S(2)}) copy-start(f32[768]{0:T(1024)} %param.27) | copy-start | bytes 9220
  206.5 277.9 %copy-start.23 = (f32[256]{0:T(256)S(1)}, f32[256]{0:T(256)}, u32[]{:S(2)}) copy-start(f32[256]{0:T(256)} %copy-done.22) | copy-start | bytes 3076
  206.6 25.1 %collective-permute-start.1 = (bf16[256,1536]{0,1:T(8,128)(2,1)}, bf16[256,1536]{0,1:T(8,128)(2,1)}, u32[]{:S(2)}, u32[]{:S(2)}) collective-permute-start(bf16[256,1536]{0,1:T(8,128)(2,1)} %get-tuple-element.1163), channel_id=1, source_target_pairs={{0,1},{1,2},{2,3},{3,4},{4,5},{5,6},{6,7},{8,9},{9,10},{10,11},{11... | collective-permute-start | bytes 2359304 | tf_op jit(solution)/shard_map/while/body/eval_jaxpr/ppermute | solution.py:17
  229.3 45.3 %collective-permute-start.2 = (bf16[256,1536]{0,1:T(8,128)(2,1)}, bf16[256,1536]{0,1:T(8,128)(2,1)}, u32[]{:S(2)}, u32[]{:S(2)}) collective-permute-start(bf16[256,1536]{0,1:T(8,128)(2,1)} %get-tuple-element.1164), channel_id=1, source_target_pairs={{0,1},{1,2},{2,3},{3,4},{4,5},{5,6},{6,7},{7,0},{8,9},{9,10},{10,1... | collective-permute-start | bytes 2359304 | tf_op jit(solution)/shard_map/while/body/eval_jaxpr/ppermute | solution.py:22
  276.9 3.5 collective-permute-start.1
  279.0 20.0 %collective-permute-start.2 = (bf16[256,1536]{0,1:T(8,128)(2,1)}, bf16[256,1536]{0,1:T(8,128)(2,1)}, u32[]{:S(2)}, u32[]{:S(2)}) collective-permute-start(bf16[256,1536]{0,1:T(8,128)(2,1)} %get-tuple-element.1164), channel_id=1, source_target_pairs={{0,1},{1,2},{2,3},{3,4},{4,5},{5,6},{6,7},{7,0},{8,9},{9,10},{10,1... | collective-permute-start | bytes 2359304 | tf_op jit(solution)/shard_map/while/body/eval_jaxpr/ppermute | solution.py:22
  301.3 4.8 collective-permute-start.1
  303.5 24.2 %collective-permute-start.2 = (bf16[256,1536]{0,1:T(8,128)(2,1)}, bf16[256,1536]{0,1:T(8,128)(2,1)}, u32[]{:S(2)}, u32[]{:S(2)}) collective-permute-start(bf16[256,1536]{0,1:T(8,128)(2,1)} %get-tuple-element.1164), channel_id=1, source_target_pairs={{0,1},{1,2},{2,3},{3,4},{4,5},{5,6},{6,7},{7,0},{8,9},{9,10},{10,1... | collective-permute-start | bytes 2359304 | tf_op jit(solution)/shard_map/while/body/eval_jaxpr/ppermute | solution.py:22
  330.0 4.2 collective-permute-start.1
  332.2 28.3 %collective-permute-start.2 = (bf16[256,1536]{0,1:T(8,128)(2,1)}, bf16[256,1536]{0,1:T(8,128)(2,1)}, u32[]{:S(2)}, u32[]{:S(2)}) collective-permute-start(bf16[256,1536]{0,1:T(8,128)(2,1)} %get-tuple-element.1164), channel_id=1, source_target_pairs={{0,1},{1,2},{2,3},{3,4},{4,5},{5,6},{6,7},{7,0},{8,9},{9,10},{10,1... | collective-permute-start | bytes 2359304 | tf_op jit(solution)/shard_map/while/body/eval_jaxpr/ppermute | solution.py:22
  362.8 3.5 collective-permute-start.1
  364.9 27.8 %collective-permute-start.2 = (bf16[256,1536]{0,1:T(8,128)(2,1)}, bf16[256,1536]{0,1:T(8,128)(2,1)}, u32[]{:S(2)}, u32[]{:S(2)}) collective-permute-start(bf16[256,1536]{0,1:T(8,128)(2,1)} %get-tuple-element.1164), channel_id=1, source_target_pairs={{0,1},{1,2},{2,3},{3,4},{4,5},{5,6},{6,7},{7,0},{8,9},{9,10},{10,1... | collective-permute-start | bytes 2359304 | tf_op jit(solution)/shard_map/while/body/eval_jaxpr/ppermute | solution.py:22
  395.0 3.5 collective-permute-start.1
  397.1 26.3 %collective-permute-start.2 = (bf16[256,1536]{0,1:T(8,128)(2,1)}, bf16[256,1536]{0,1:T(8,128)(2,1)}, u32[]{:S(2)}, u32[]{:S(2)}) collective-permute-start(bf16[256,1536]{0,1:T(8,128)(2,1)} %get-tuple-element.1164), channel_id=1, source_target_pairs={{0,1},{1,2},{2,3},{3,4},{4,5},{5,6},{6,7},{7,0},{8,9},{9,10},{10,1... | collective-permute-start | bytes 2359304 | tf_op jit(solution)/shard_map/while/body/eval_jaxpr/ppermute | solution.py:22
  425.7 3.5 collective-permute-start.1
  427.9 26.3 %collective-permute-start.2 = (bf16[256,1536]{0,1:T(8,128)(2,1)}, bf16[256,1536]{0,1:T(8,128)(2,1)}, u32[]{:S(2)}, u32[]{:S(2)}) collective-permute-start(bf16[256,1536]{0,1:T(8,128)(2,1)} %get-tuple-element.1164), channel_id=1, source_target_pairs={{0,1},{1,2},{2,3},{3,4},{4,5},{5,6},{6,7},{7,0},{8,9},{9,10},{10,1... | collective-permute-start | bytes 2359304 | tf_op jit(solution)/shard_map/while/body/eval_jaxpr/ppermute | solution.py:22
  456.5 27.0 %collective-permute-start.3 = (bf16[256,1536]{0,1:T(8,128)(2,1)}, bf16[256,1536]{0,1:T(8,128)(2,1)S(1)}, u32[]{:S(2)}, u32[]{:S(2)}) collective-permute-start(bf16[256,1536]{0,1:T(8,128)(2,1)} %get-tuple-element.671), channel_id=1, source_target_pairs={{0,1},{1,2},{2,3},{3,4},{4,5},{5,6},{6,7},{7,0},{8,9},{9,10},{10,1... | collective-permute-start | bytes 2359304 | tf_op jit(solution)/shard_map/ppermute | solution.py:22
  457.7 25.8 %copy-start.11 = (bf16[256,12,64]{0,2,1:T(8,128)(2,1)}, bf16[256,12,64]{0,2,1:T(8,128)(2,1)S(1)}, u32[]{:S(2)}) copy-start(bf16[256,12,64]{0,2,1:T(8,128)(2,1)S(1)} %convert.5) | copy-start | bytes 1179652
  483.5 0.9 copy-start.12
  489.7 0.7 copy-start.17
  489.7 0.7 copy-start.20
  489.7 263.7 %reduce-scatter.9.cloned.1.call-start = ((), (), s32[]{:S(2)}) async-start(), calls=%async_computation.6 | async-start | bytes 9732096 | tf_op jit(solution)/shard_map/reduce_scatter | solution.py:257
  497.3 398.1 %reduce-scatter.11.cloned.1.call-start = ((), (), s32[]{:S(2)}) async-start(), calls=%async_computation.7 | async-start | bytes 9732096 | tf_op jit(solution)/shard_map/reduce_scatter | solution.py:258
  506.2 3.3 copy-start.35
  506.2 3.3 copy-start.3
  506.2 3.3 copy-start.25
  509.5 1.1 copy-start.9
  509.5 1.1 copy-start.32
Sparse Core Ops, SparseCore 0:
  186.8 155.3 reduce-scatter.6
  489.8 122.1 reduce-scatter.4
  618.5 134.8 reduce-scatter.8
  760.7 134.5 reduce-scatter.10
where the time goes:
time: 912 us; the launch traced here: 902 us
  waiting for transfers between devices  534 us (59%)
  starting transfers between devices  139 us (15%)
  matrix products  60.1 us (7%)
  local copies, waits for them, and re-layouts  59.9 us (7%)
  blocking collectives  42 us (5%)
  other arithmetic  39.7 us (4%)
  between operations  16 us (2%)
  loops' own time  10.8 us (1%)
    ppermute x8, waiting for transfers between devices, shifted(): lax.ppermute(array, axis, [(i, (i + by) % devices) for i in range(devices)])  196 us
    reduce_scatter x1, waiting for transfers between devices, per_device(): lax.psum_scatter(grad_w_down, ('grp', 'seq'), scatter_dimension=0, tiled=...  142 us
    reduce_scatter x1, waiting for transfers between devices, per_device(): lax.psum_scatter(grad_w_up, ('grp', 'seq'), scatter_dimension=0, tiled=True)  141 us
    ppermute x14, starting transfers between devices, passed_along(): return lax.ppermute(array, axis, pairs)  134 us
    reduce_scatter x1, waiting for transfers between devices, per_device(): lax.psum_scatter(grad_w_qkv, ('grp', 'seq'), scatter_dimension=0, tiled=T...  47.8 us
    unnamed x1, blocking collectives  42 us
    while x14, local copies, waits for them, and re-layouts  28.9 us
    dot_general x4, matrix products, contract_rows(): lax.dot_general(left, right, (((0,), (0,)), ((), ())), preferred_element_...  21.9 us
  transfers between devices with their start and end apart: 26, of which 22 were waited for; matrix products, arithmetic and copies ran while one was open for 10% of the time, Pallas kernels for 0%

commit v1 on v0

--- a/solution.py
+++ b/solution.py
@@ -1,11 +1,16 @@
+import functools
+
 import jax
 import jax.numpy as jnp
 from jax import lax
+from jax.experimental import pallas as pl
+from jax.experimental.pallas import tpu as pltpu
 from jax.sharding import PartitionSpec as P
 
 D = 768
 HEADS = 12
 HEAD_DIM = 64
+MESH = pl.DeviceIdType.MESH
 
 
 epsilon = 1e-05
@@ -120,7 +125,166 @@
     return (grad_query, grad_pair)
 
 
+def rs_kernel(shapes, *refs):
+    n = len(shapes)
+    ins, small_in = refs[:n], refs[n]
+    outs, small_out = refs[n + 1 : 2 * n + 1], refs[2 * n + 1]
+    scratch = refs[2 * n + 2 :]
+    first, held, second, mine, third = (scratch[i * n : (i + 1) * n] for i in range(5))
+    small_a, small_b, small_c = scratch[5 * n : 5 * n + 3]
+    send_sems, recv_sems = scratch[5 * n + 3 :]
+
+    grp, seq = lax.axis_index("grp"), lax.axis_index("seq")
+    zed, core = seq // 2, seq % 2
+    sibling = (grp, zed * 2 + 1 - core)
+    across = [((grp // 2 + k // 2) % 2) * 2 + (grp % 2 + k % 2) % 2 for k in range(4)]
+    along = [(zed + k) % 4 for k in range(4)]
+    back = [(zed + 4 - k) % 4 for k in range(4)]
+
+    barrier = pltpu.get_barrier_semaphore()
+    partners = [sibling]
+    partners += [(across[k], seq) for k in (1, 2, 3)]
+    partners += [(grp, along[k] * 2 + core) for k in (1, 2, 3)]
+    for partner in partners:
+        pl.semaphore_signal(barrier, inc=1, device_id=partner, device_id_type=MESH)
+    pl.semaphore_wait(barrier, len(partners))
+
+    def send(src, dst, slot, target):
+        copy = pltpu.make_async_remote_copy(
+            src_ref=src, dst_ref=dst, send_sem=send_sems.at[slot], recv_sem=recv_sems.at[slot],
+            device_id=target, device_id_type=MESH,
+        )
+        copy.start()
+        return copy
+
+    def rows(start, count):
+        return pl.ds(pl.multiple_of(start, 16), count)
+
+    copies = {}
+    slot = 0
+    copies["s0"] = send(small_in, small_a.at[1 - 0], slot, sibling)
+    slot += 1
+    for a, (r, c) in enumerate(shapes):
+        for k in (1, 2, 3, 0):
+            at = rows(across[k] * (r // 4), r // 4)
+            cols = pl.ds(pl.multiple_of((1 - core) * (c // 2), 128), c // 2)
+            copies["a", a, k] = send(ins[a].at[at, cols], first[a].at[at, :], slot, sibling)
+            slot += 1
+
+    copies["s0"].wait()
+    small_a[0] = small_in[...] + small_a[1]
+    small_b[pl.ds(grp, 1)] = small_a[0:1]
+    for k in (1, 2, 3):
+        copies["s1", k] = send(small_a.at[0], small_b.at[grp], slot, (across[k], seq))
+        slot += 1
+
+    for a, (r, c) in enumerate(shapes):
+        half = pl.ds(pl.multiple_of(core * (c // 2), 128), c // 2)
+        for k in (1, 2, 3):
+            base = across[k] * (r // 4)
+            copies["a", a, k].wait_recv()
+
+            def add(i, _):
+                at = rows(base + i * 16, 16)
+                first[a][at, :] = (
+                    ins[a][at, half].astype(jnp.float32) + first[a][at, :].astype(jnp.float32)
+                ).astype(jnp.bfloat16)
+                return 0
+
+            lax.fori_loop(0, r // 64, add, 0)
+            copies["b", a, k] = send(
+                first[a].at[rows(base, r // 4), :], second[a].at[k - 1], slot, (across[k], seq)
+            )
+            slot += 1
+
+    for k in (1, 2, 3):
+        copies["s1", k].wait()
+    small_c[pl.ds(zed, 1)] = (small_b[0:1] + small_b[1:2]) + (small_b[2:3] + small_b[3:4])
+    for k in (1, 2, 3):
+        copies["s2", k] = send(small_c.at[zed], small_c.at[zed], slot, (grp, along[k] * 2 + core))
+        slot += 1
+
+    for a, (r, c) in enumerate(shapes):
+        half = pl.ds(pl.multiple_of(core * (c // 2), 128), c // 2)
+        base = across[0] * (r // 4)
+        copies["a", a, 0].wait_recv()
+        for k in (1, 2, 3):
+            copies["b", a, k].wait_recv()
+
+        def gather(i, _):
+            at = rows(base + i * 16, 16)
+            here = rows(i * 16, 16)
+            total = ins[a][at, half].astype(jnp.float32) + first[a][at, :].astype(jnp.float32)
+            for j in range(3):
+                total = total + second[a][j, here, :].astype(jnp.float32)
+            held[a][here, :] = total.astype(jnp.bfloat16)
+            return 0
+
+        lax.fori_loop(0, r // 64, gather, 0)
+        for k in (1, 2, 3):
+            copies["c", a, k] = send(
+                held[a].at[rows(along[k] * (r // 16), r // 16), :],
+                third[a].at[k - 1],
+                slot,
+                (grp, along[k] * 2 + core),
+            )
+            slot += 1
+
+    for k in (1, 2, 3):
+        copies["s2", k].wait()
+    small_out[...] = (small_c[0] + small_c[1]) + (small_c[2] + small_c[3])
+
+    for a, (r, c) in enumerate(shapes):
+        half = pl.ds(pl.multiple_of(core * (c // 2), 128), c // 2)
+        for k in (1, 2, 3):
+            copies["c", a, k].wait_recv()
+        for part in range(2):
+            total = held[a][rows(zed * (r // 16), r // 16), :].astype(jnp.float32)
+            for j in range(3):
+                total = total + third[a][j].astype(jnp.float32)
+        mine[a][...] = total
+        count = r // 32
+        copies["d", a] = send(
+            mine[a].at[pl.ds(pl.multiple_of((1 - core) * count, 8), count), :],
+            outs[a].at[:, half], slot, sibling,
+        )
+        slot += 1
+        outs[a][:, half] = mine[a][pl.ds(pl.multiple_of(core * count, 8), count), :]
+    for key, copy in copies.items():
+        if key == "s0" or key[0] in ("s1", "s2"):
+            continue
+        copy.wait_send()
+        if key[0] == "d":
+            copy.wait_recv()
+
+
+def reduce_scatter(grads, small):
+    shapes = tuple(g.shape for g in grads)
+    vmem = pl.BlockSpec(memory_space=pltpu.VMEM)
+    bf16, f32 = jnp.bfloat16, jnp.float32
+    copies = 1 + 3 + 3 + len(shapes) * (4 + 3 + 3 + 1)
+    scratch = [pltpu.VMEM((r, c // 2), bf16) for r, c in shapes]
+    scratch += [pltpu.VMEM((r // 4, c // 2), bf16) for r, c in shapes]
+    scratch += [pltpu.VMEM((3, r // 4, c // 2), bf16) for r, c in shapes]
+    scratch += [pltpu.VMEM((r // 16, c // 2), f32) for r, c in shapes]
+    scratch += [pltpu.VMEM((3, r // 16, c // 2), bf16) for r, c in shapes]
+    scratch += [pltpu.VMEM((count,) + small.shape, f32) for count in (2, 4, 4)]
+    scratch += [pltpu.SemaphoreType.DMA((copies,)), pltpu.SemaphoreType.DMA((copies,))]
+    return pl.pallas_call(
+        functools.partial(rs_kernel, shapes),
+        out_shape=[jax.ShapeDtypeStruct((r // 32, c), f32) for r, c in shapes]
+        + [jax.ShapeDtypeStruct(small.shape, f32)],
+        in_specs=[vmem] * (len(shapes) + 1),
+        out_specs=[vmem] * (len(shapes) + 1),
+        scratch_shapes=scratch,
+        compiler_params=pltpu.CompilerParams(
+            collective_id=0, has_side_effects=True, vmem_limit_bytes=60 * 2**20
+        ),
+    )(*grads, small)
+
+
 def per_device(
+    planned,
     block_input,
     out_grad,
     seq_span,
@@ -179,16 +343,12 @@
     mlp_out = jnp.dot(activated, w_down, preferred_element_type=jnp.float32)
     output = middle + mlp_out
     valid_rows = ((query_pos >= seq_first) & (query_pos < seq_limit)).astype(jnp.float32)[:, None]
-    rms_parts = lax.psum(
-        (
-            jnp.sum(valid_rows * output * output),
-            jnp.sum(valid_rows * attn_out * attn_out),
-            jnp.sum(valid_rows * mlp_out * mlp_out),
-            jnp.sum(valid_rows) * feat_width,
-        ),
-        ("grp", "seq"),
-    )
-    rms_stats = jnp.sqrt(jnp.stack([rms_parts[0], rms_parts[1], rms_parts[2]]) / rms_parts[3])
+    rms_terms = (
+        jnp.sum(valid_rows * output * output),
+        jnp.sum(valid_rows * attn_out * attn_out),
+        jnp.sum(valid_rows * mlp_out * mlp_out),
+        jnp.sum(valid_rows) * feat_width,
+    )
     grad_w_down = contract_rows(activated, out_grad)
     grad_activated = contract_cols(out_grad, w_down)
     _, gelu_pull = jax.vjp(lambda pre_act: jax.nn.gelu(pre_act, approximate=True), up_proj)
@@ -247,16 +407,32 @@
     _, norm_pull_one = jax.vjp(layer_norm, inputs, ln1_gain, ln1_bias)
     grad_in_norm, grad_gain_one, grad_bias_one = norm_pull_one(grad_norm_one)
     input_grad = (grad_middle + grad_in_norm).astype(jnp.bfloat16)
-    summed = (
-        lax.psum_scatter(grad_gain_one, ("grp", "seq"), scatter_dimension=0, tiled=True),
-        lax.psum_scatter(grad_bias_one, ("grp", "seq"), scatter_dimension=0, tiled=True),
-        lax.psum_scatter(grad_w_qkv, ("grp", "seq"), scatter_dimension=0, tiled=True),
-        lax.psum_scatter(grad_w_out, ("grp", "seq"), scatter_dimension=0, tiled=True),
-        lax.psum_scatter(grad_gain_two, ("grp", "seq"), scatter_dimension=0, tiled=True),
-        lax.psum_scatter(grad_bias_two, ("grp", "seq"), scatter_dimension=0, tiled=True),
-        lax.psum_scatter(grad_w_up, ("grp", "seq"), scatter_dimension=0, tiled=True),
-        lax.psum_scatter(grad_w_down, ("grp", "seq"), scatter_dimension=0, tiled=True),
-    )
+    if planned:
+        bf16 = jnp.bfloat16
+        grads = [g.astype(bf16) for g in (grad_w_qkv, grad_w_out, grad_w_up, grad_w_down)]
+        rms_row = jnp.pad(jnp.stack(rms_terms), (0, feat_width - 4))
+        small = jnp.stack(
+            [grad_gain_one, grad_bias_one, grad_gain_two, grad_bias_two, rms_row] + [rms_row] * 3
+        )
+        *sums, small = reduce_scatter(grads, small)
+        rms_stats = jnp.sqrt(small[4, :3] / small[4, 3])
+        count = feat_width // (seq_count * lax.axis_size("grp"))
+        place = (lax.axis_index("grp") * seq_count + seq_index) * count
+        vecs = [lax.dynamic_slice(small[i], (place,), (count,)) for i in range(4)]
+        summed = (vecs[0], vecs[1], sums[0], sums[1], vecs[2], vecs[3], sums[2], sums[3])
+    else:
+        rms_parts = lax.psum(rms_terms, ("grp", "seq"))
+        rms_stats = jnp.sqrt(jnp.stack(rms_parts[:3]) / rms_parts[3])
+        summed = (
+            lax.psum_scatter(grad_gain_one, ("grp", "seq"), scatter_dimension=0, tiled=True),
+            lax.psum_scatter(grad_bias_one, ("grp", "seq"), scatter_dimension=0, tiled=True),
+            lax.psum_scatter(grad_w_qkv, ("grp", "seq"), scatter_dimension=0, tiled=True),
+            lax.psum_scatter(grad_w_out, ("grp", "seq"), scatter_dimension=0, tiled=True),
+            lax.psum_scatter(grad_gain_two, ("grp", "seq"), scatter_dimension=0, tiled=True),
+            lax.psum_scatter(grad_bias_two, ("grp", "seq"), scatter_dimension=0, tiled=True),
+            lax.psum_scatter(grad_w_up, ("grp", "seq"), scatter_dimension=0, tiled=True),
+            lax.psum_scatter(grad_w_down, ("grp", "seq"), scatter_dimension=0, tiled=True),
+        )
     return (
         output.astype(jnp.bfloat16),
         input_grad,
@@ -286,8 +462,9 @@
         P(),
         P(),
     )
+    planned = mesh.shape["grp"] == 4 and mesh.shape["seq"] == 8
     return jax.shard_map(
-        per_device,
+        functools.partial(per_device, planned),
         mesh=mesh,
         in_specs=placed,
         out_specs=(

time: 912 us -> 618 us (0.68)
  waiting for transfers between devices: 534 us -> 177 us
  Pallas kernels: 0 us -> 116 us
  blocking collectives: 42 us -> 0 us
  between operations: 16 us -> 2.76 us
    reduce_scatter x4 -> x0, waiting for transfers between devices: 331 us -> none  [the longest x1 142 us: per_device(): lax.psum_scatter(grad_w_down, ('grp', 'seq'), scatter_dimension=0, tiled=...]
    pallas_call x0 -> x1, Pallas kernels: none -> 116 us  [reduce_scatter(): pl.pallas_call(functools.partial(rs_kernel, shapes), out_shape=[jax.Shape...]
    unnamed x1 -> x0, blocking collectives: 42 us -> none
    ppermute x8, waiting for transfers between devices: 196 us -> 169 us  [shifted(): lax.ppermute(array, axis, [(i, (i + by) % devices) for i in range(devices)])]
  transfers between devices with their start and end apart: 26 -> 22, of which waited for: 22 -> 20; matrix products, arithmetic and copies ran while one was open for 10% -> 6% of each run, Pallas kernels for 0% -> 0%
where the time goes in v1:
time: 618 us; the launch traced here: 608 us
  waiting for transfers between devices  177 us (29%)
  starting transfers between devices  141 us (23%)
  Pallas kernels  116 us (19%)
  local copies, waits for them, and re-layouts  65.5 us (11%)
  matrix products  55.2 us (9%)
  other arithmetic  40.3 us (7%)
  loops' own time  10.2 us (2%)
    ppermute x8, waiting for transfers between devices, shifted(): lax.ppermute(array, axis, [(i, (i + by) % devices) for i in range(devices)])  169 us
    ppermute x14, starting transfers between devices, passed_along(): return lax.ppermute(array, axis, pairs)  135 us
    pallas_call x1, Pallas kernels, reduce_scatter(): pl.pallas_call(functools.partial(rs_kernel, shapes), out_shape=[jax.Shape...  116 us
    while x14, local copies, waits for them, and re-layouts  29 us
    dot_general x4, matrix products, contract_rows(): lax.dot_general(left, right, (((0,), (0,)), ((), ())), preferred_element_...  19 us
    add x7, other arithmetic, backward_hop(): return (moving, grad_acc + new_terms, grad_run)  15.9 us
  transfers between devices with their start and end apart: 22, of which 20 were waited for; matrix products, arithmetic and copies ran while one was open for 6% of the time, Pallas kernels for 0%

profile of v1, /device:TPU:0, one launch (start us, length us, event | category | flops | bytes accessed | tf_op | source)
XLA Modules:
  0.0 608.1 jit_solution(14060427268112341228)
XLA Ops:
  3.8 2.2 convolution_convert_fusion.3
  8.3 2.3 copy.66
  10.6 2.1 copy.92
  16.4 13.5 %conditional.4 = (f32[256,12]{0,1:T(8,128)S(1)}, f32[256,12,64]{0,2,1:T(8,128)}) conditional(s32[]{:T(128)} %convert_element_type.131, () %tuple.90, (s32[]{:T(128)}, s32[256]{0:T(256)}, s32[]{:T(128)}, s32[]{:T(128)}, bf16[256,1536]{1,0:T(8,128)(2,1)}, /*index=5*/bf16[256,12,64]{0,2,1:T(8,128)(2,1)}) %tuple.195), branch_computations={%region_2.0_spmd, %region_3.5_spmd} | conditional | flops 211090432 | bytes 11879484 | solution.py:315
  19.8 2.3 copy.65
  23.3 3.0 fusion.10
  26.3 3.1 fusion.13
  29.9 126.3 %while.43 = (s32[]{:T(128)}, bf16[256,1536]{0,1:T(8,128)(2,1)}, f32[256,12]{0,1:T(8,128)S(1)}, f32[256,12,64]{0,2,1:T(8,128)}, s32[]{:T(128)}, /*index=5*/s32[]{...) while((s32[]{:T(128)}, bf16[256,1536]{0,1:T(8,128)(2,1)}, ...), condition=%wide.region_9.10_spmd.clone, body=%wide.region_5.9_spmd.clone.sunk | while | flops 211290384 | bytes 15588812 | solution.py:336
  29.9 3.3 collective-permute-start
  35.1 2.1 copy.100
  37.2 23.0 %collective-permute-start = (bf16[256,1536]{0,1:T(8,128)(2,1)}, bf16[256,1536]{0,1:T(8,128)(2,1)}, u32[]{:S(2)}, u32[]{:S(2)}) collective-permute-start(bf16[256,1536]{0,1:T(8,128)(2,1)} %get-tuple-element.1118), channel_id=1, source_target_pairs={{0,1},{1,2},{2,3},{3,4},{4,5},{5,6},{6,7},{8,9},{9,10},{10,11},{11... | collective-permute-start | bytes 2359304 | tf_op jit(solution)/shard_map/while/body/eval_jaxpr/ppermute | solution.py:22
  62.1 2.1 copy.100
  64.2 12.3 %collective-permute-start = (bf16[256,1536]{0,1:T(8,128)(2,1)}, bf16[256,1536]{0,1:T(8,128)(2,1)}, u32[]{:S(2)}, u32[]{:S(2)}) collective-permute-start(bf16[256,1536]{0,1:T(8,128)(2,1)} %get-tuple-element.1118), channel_id=1, source_target_pairs={{0,1},{1,2},{2,3},{3,4},{4,5},{5,6},{6,7},{8,9},{9,10},{10,11},{11... | collective-permute-start | bytes 2359304 | tf_op jit(solution)/shard_map/while/body/eval_jaxpr/ppermute | solution.py:22
  78.3 2.1 copy.100
  80.4 22.8 %collective-permute-start = (bf16[256,1536]{0,1:T(8,128)(2,1)}, bf16[256,1536]{0,1:T(8,128)(2,1)}, u32[]{:S(2)}, u32[]{:S(2)}) collective-permute-start(bf16[256,1536]{0,1:T(8,128)(2,1)} %get-tuple-element.1118), channel_id=1, source_target_pairs={{0,1},{1,2},{2,3},{3,4},{4,5},{5,6},{6,7},{8,9},{9,10},{10,11},{11... | collective-permute-start | bytes 2359304 | tf_op jit(solution)/shard_map/while/body/eval_jaxpr/ppermute | solution.py:22
  105.1 2.1 copy.100
  107.2 12.3 %collective-permute-start = (bf16[256,1536]{0,1:T(8,128)(2,1)}, bf16[256,1536]{0,1:T(8,128)(2,1)}, u32[]{:S(2)}, u32[]{:S(2)}) collective-permute-start(bf16[256,1536]{0,1:T(8,128)(2,1)} %get-tuple-element.1118), channel_id=1, source_target_pairs={{0,1},{1,2},{2,3},{3,4},{4,5},{5,6},{6,7},{8,9},{9,10},{10,11},{11... | collective-permute-start | bytes 2359304 | tf_op jit(solution)/shard_map/while/body/eval_jaxpr/ppermute | solution.py:22
  121.4 2.1 copy.100
  123.4 12.5 %collective-permute-start = (bf16[256,1536]{0,1:T(8,128)(2,1)}, bf16[256,1536]{0,1:T(8,128)(2,1)}, u32[]{:S(2)}, u32[]{:S(2)}) collective-permute-start(bf16[256,1536]{0,1:T(8,128)(2,1)} %get-tuple-element.1118), channel_id=1, source_target_pairs={{0,1},{1,2},{2,3},{3,4},{4,5},{5,6},{6,7},{8,9},{9,10},{10,11},{11... | collective-permute-start | bytes 2359304 | tf_op jit(solution)/shard_map/while/body/eval_jaxpr/ppermute | solution.py:22
  137.9 2.1 copy.100
  139.9 12.3 %collective-permute-start = (bf16[256,1536]{0,1:T(8,128)(2,1)}, bf16[256,1536]{0,1:T(8,128)(2,1)}, u32[]{:S(2)}, u32[]{:S(2)}) collective-permute-start(bf16[256,1536]{0,1:T(8,128)(2,1)} %get-tuple-element.1118), channel_id=1, source_target_pairs={{0,1},{1,2},{2,3},{3,4},{4,5},{5,6},{6,7},{8,9},{9,10},{10,11},{11... | collective-permute-start | bytes 2359304 | tf_op jit(solution)/shard_map/while/body/eval_jaxpr/ppermute | solution.py:22
  154.1 2.1 copy.100
  157.5 2.1 fusion.113
  161.8 3.9 fusion.122
  165.7 5.1 fusion.80
  173.0 3.8 fusion.92
  181.4 15.2 %conditional.5 = (f32[256,12,64]{0,2,1:T(8,128)}, bf16[256,1536]{0,1:T(8,128)(2,1)}) conditional(s32[]{:T(128)} %convert_element_type.131, () %tuple.93, (bf16[256,1536]{1,0:T(8,128)(2,1)}, bf16[256,12,64]{0,2,1:T(8,128)(2,1)}, s32[]{:T(128)}, s32[256]{0:T(256)}, s32[]{:T(128)}, /*index=5*/s32[]{:T(128)}, bf16[256,12,64]{0,2,1:T(8,128)(2,1)}, ...), branch_computations={%region_15.16_spmd, %region_16.17_spmd} | conditional | flops 523110400 | bytes 26612880 | solution.py:385
  181.5 2.3 copy.68
  188.2 3.2 fusion.48
  192.7 2.2 fusion.49
  196.6 244.6 %while.44 = (s32[]{:T(128)}, bf16[256,1536]{0,1:T(8,128)(2,1)}, bf16[256,1536]{0,1:T(8,128)(2,1)}, f32[256,12,64]{0,2,1:T(8,128)}, s32[]{:T(128)}, /*index=5*/s3...) while((s32[]{:T(128)}, bf16[256,1536]{0,1:T(8,128)(2,1)}, ...), condition=%wide.region_20.21_spmd.clone, body=%wide.region_17.20_spmd.clone.sunk | while | flops 523110656 | bytes 39194184 | solution.py:398
  196.7 22.8 %collective-permute-start.1 = (bf16[256,1536]{0,1:T(8,128)(2,1)}, bf16[256,1536]{0,1:T(8,128)(2,1)}, u32[]{:S(2)}, u32[]{:S(2)}) collective-permute-start(bf16[256,1536]{0,1:T(8,128)(2,1)} %get-tuple-element.1169), channel_id=1, source_target_pairs={{0,1},{1,2},{2,3},{3,4},{4,5},{5,6},{6,7},{8,9},{9,10},{10,11},{11... | collective-permute-start | bytes 2359304 | tf_op jit(solution)/shard_map/while/body/eval_jaxpr/ppermute | solution.py:22
  221.9 2.1 copy.116
  224.0 40.7 %collective-permute-done.2 = bf16[256,1536]{0,1:T(8,128)(2,1)} collective-permute-done((bf16[256,1536]{0,1:T(8,128)(2,1)}, bf16[256,1536]{0,1:T(8,128)(2,1)}, u32[]{:S(2)}, u32[]{:S(2)}) %collective-permute-start.2) | collective-permute-done | bytes 786464 | tf_op jit(solution)/shard_map/while/body/eval_jaxpr/ppermute | solution.py:27
  264.7 2.3 convert_add_fusion.4
  267.0 2.2 collective-permute-start.1
  270.7 2.1 copy.116
  272.7 13.7 %collective-permute-done.2 = bf16[256,1536]{0,1:T(8,128)(2,1)} collective-permute-done((bf16[256,1536]{0,1:T(8,128)(2,1)}, bf16[256,1536]{0,1:T(8,128)(2,1)}, u32[]{:S(2)}, u32[]{:S(2)}) %collective-permute-start.2) | collective-permute-done | bytes 786464 | tf_op jit(solution)/shard_map/while/body/eval_jaxpr/ppermute | solution.py:27
  286.4 2.3 convert_add_fusion.4
  288.7 2.2 collective-permute-start.1
  290.9 4.5 collective-permute-start.2
  298.3 17.5 %collective-permute-done.2 = bf16[256,1536]{0,1:T(8,128)(2,1)} collective-permute-done((bf16[256,1536]{0,1:T(8,128)(2,1)}, bf16[256,1536]{0,1:T(8,128)(2,1)}, u32[]{:S(2)}, u32[]{:S(2)}) %collective-permute-start.2) | collective-permute-done | bytes 786464 | tf_op jit(solution)/shard_map/while/body/eval_jaxpr/ppermute | solution.py:27
  315.8 2.3 convert_add_fusion.4
  318.1 2.2 collective-permute-start.1
  321.7 2.1 copy.116
  323.8 22.8 %collective-permute-done.2 = bf16[256,1536]{0,1:T(8,128)(2,1)} collective-permute-done((bf16[256,1536]{0,1:T(8,128)(2,1)}, bf16[256,1536]{0,1:T(8,128)(2,1)}, u32[]{:S(2)}, u32[]{:S(2)}) %collective-permute-start.2) | collective-permute-done | bytes 786464 | tf_op jit(solution)/shard_map/while/body/eval_jaxpr/ppermute | solution.py:27
  346.6 2.3 convert_add_fusion.4
  348.9 2.2 collective-permute-start.1
  354.6 22.8 %collective-permute-done.2 = bf16[256,1536]{0,1:T(8,128)(2,1)} collective-permute-done((bf16[256,1536]{0,1:T(8,128)(2,1)}, bf16[256,1536]{0,1:T(8,128)(2,1)}, u32[]{:S(2)}, u32[]{:S(2)}) %collective-permute-start.2) | collective-permute-done | bytes 786464 | tf_op jit(solution)/shard_map/while/body/eval_jaxpr/ppermute | solution.py:27
  377.4 2.3 convert_add_fusion.4
  379.6 2.2 collective-permute-start.1
  385.4 22.8 %collective-permute-done.2 = bf16[256,1536]{0,1:T(8,128)(2,1)} collective-permute-done((bf16[256,1536]{0,1:T(8,128)(2,1)}, bf16[256,1536]{0,1:T(8,128)(2,1)}, u32[]{:S(2)}, u32[]{:S(2)}) %collective-permute-start.2) | collective-permute-done | bytes 786464 | tf_op jit(solution)/shard_map/while/body/eval_jaxpr/ppermute | solution.py:27
  408.2 2.3 convert_add_fusion.4
  410.4 2.2 collective-permute-start.1
  416.2 22.8 %collective-permute-done.2 = bf16[256,1536]{0,1:T(8,128)(2,1)} collective-permute-done((bf16[256,1536]{0,1:T(8,128)(2,1)}, bf16[256,1536]{0,1:T(8,128)(2,1)}, u32[]{:S(2)}, u32[]{:S(2)}) %collective-permute-start.2) | collective-permute-done | bytes 786464 | tf_op jit(solution)/shard_map/while/body/eval_jaxpr/ppermute | solution.py:27
  438.9 2.3 convert_add_fusion.4
  441.5 5.4 convolution_convert_fusion.1.refs_2_
  453.3 2.6 convolution_convert_fusion.4.refs_1_
  455.9 6.5 %convolution_convert_fusion.refs_3_ = bf16[3072,768]{1,0:T(8,128)(2,1)} fusion(bf16[256,768]{1,0:T(8,128)(2,1)} %param.24, f32[256,3072]{1,0:T(8,128)} %copy-done.47), kind=kOutput, calls=%fused_computation.101 | convolution fusion | flops 1217396736 | bytes 8257536 | tf_op jit(solution)/shard_map/dot_general | solution.py:38
  462.4 6.2 %collective-permute-done.3 = bf16[256,1536]{0,1:T(8,128)(2,1)} collective-permute-done((bf16[256,1536]{0,1:T(8,128)(2,1)}, bf16[256,1536]{0,1:T(8,128)(2,1)}, u32[]{:S(2)}, u32[]{:S(2)}) %collective-permute-start.3) | collective-permute-done | bytes 786464 | tf_op jit(solution)/shard_map/ppermute | solution.py:27
  468.7 2.4 fusion.110
  474.7 4.5 convolution_convert_fusion.2.refs_0_
  479.3 115.8 %shard_map.194 = (f32[24,2304]{1,0:T(8,128)}, f32[24,768]{1,0:T(8,128)}, f32[24,3072]{1,0:T(8,128)}, f32[96,768]{1,0:T(8,128)}, f32[8,768]{1,0:T(8,128)}) custom-call(bf16[768,2304]{1,0:T(8,128)(2,1)} %convolution_convert_fusion.2.refs_0_, bf16[768,768]{1,0:T(8,128)(2,1)} %convolution_convert_fusion.4.refs_1_, ...), custom_call_target="tpu_custom_call" | custom-call | tf_op jit(solution)/shard_map/pallas_call | solution.py:273
  597.3 2.6 add_convert_fusion
  (216 shorter events, 73.7 us)
Async XLA Ops:
  0.6 3.1 copy-start
  1.9 4.0 copy-start.26
  3.8 2.2 copy-start.28
  3.8 3.9 copy-start.46
  23.3 3.0 copy-start.25
  29.9 4.6 collective-permute-start
  37.2 24.3 %collective-permute-start = (bf16[256,1536]{0,1:T(8,128)(2,1)}, bf16[256,1536]{0,1:T(8,128)(2,1)}, u32[]{:S(2)}, u32[]{:S(2)}) collective-permute-start(bf16[256,1536]{0,1:T(8,128)(2,1)} %get-tuple-element.1118), channel_id=1, source_target_pairs={{0,1},{1,2},{2,3},{3,4},{4,5},{5,6},{6,7},{8,9},{9,10},{10,11},{11... | collective-permute-start | bytes 2359304 | tf_op jit(solution)/shard_map/while/body/eval_jaxpr/ppermute | solution.py:22
  64.2 13.6 %collective-permute-start = (bf16[256,1536]{0,1:T(8,128)(2,1)}, bf16[256,1536]{0,1:T(8,128)(2,1)}, u32[]{:S(2)}, u32[]{:S(2)}) collective-permute-start(bf16[256,1536]{0,1:T(8,128)(2,1)} %get-tuple-element.1118), channel_id=1, source_target_pairs={{0,1},{1,2},{2,3},{3,4},{4,5},{5,6},{6,7},{8,9},{9,10},{10,11},{11... | collective-permute-start | bytes 2359304 | tf_op jit(solution)/shard_map/while/body/eval_jaxpr/ppermute | solution.py:22
  80.4 24.1 %collective-permute-start = (bf16[256,1536]{0,1:T(8,128)(2,1)}, bf16[256,1536]{0,1:T(8,128)(2,1)}, u32[]{:S(2)}, u32[]{:S(2)}) collective-permute-start(bf16[256,1536]{0,1:T(8,128)(2,1)} %get-tuple-element.1118), channel_id=1, source_target_pairs={{0,1},{1,2},{2,3},{3,4},{4,5},{5,6},{6,7},{8,9},{9,10},{10,11},{11... | collective-permute-start | bytes 2359304 | tf_op jit(solution)/shard_map/while/body/eval_jaxpr/ppermute | solution.py:22
  107.2 13.6 %collective-permute-start = (bf16[256,1536]{0,1:T(8,128)(2,1)}, bf16[256,1536]{0,1:T(8,128)(2,1)}, u32[]{:S(2)}, u32[]{:S(2)}) collective-permute-start(bf16[256,1536]{0,1:T(8,128)(2,1)} %get-tuple-element.1118), channel_id=1, source_target_pairs={{0,1},{1,2},{2,3},{3,4},{4,5},{5,6},{6,7},{8,9},{9,10},{10,11},{11... | collective-permute-start | bytes 2359304 | tf_op jit(solution)/shard_map/while/body/eval_jaxpr/ppermute | solution.py:22
  123.4 13.9 %collective-permute-start = (bf16[256,1536]{0,1:T(8,128)(2,1)}, bf16[256,1536]{0,1:T(8,128)(2,1)}, u32[]{:S(2)}, u32[]{:S(2)}) collective-permute-start(bf16[256,1536]{0,1:T(8,128)(2,1)} %get-tuple-element.1118), channel_id=1, source_target_pairs={{0,1},{1,2},{2,3},{3,4},{4,5},{5,6},{6,7},{8,9},{9,10},{10,11},{11... | collective-permute-start | bytes 2359304 | tf_op jit(solution)/shard_map/while/body/eval_jaxpr/ppermute | solution.py:22
  139.9 13.6 %collective-permute-start = (bf16[256,1536]{0,1:T(8,128)(2,1)}, bf16[256,1536]{0,1:T(8,128)(2,1)}, u32[]{:S(2)}, u32[]{:S(2)}) collective-permute-start(bf16[256,1536]{0,1:T(8,128)(2,1)} %get-tuple-element.1118), channel_id=1, source_target_pairs={{0,1},{1,2},{2,3},{3,4},{4,5},{5,6},{6,7},{8,9},{9,10},{10,11},{11... | collective-permute-start | bytes 2359304 | tf_op jit(solution)/shard_map/while/body/eval_jaxpr/ppermute | solution.py:22
  156.2 5.5 copy-start.8
  157.5 2.3 copy-start.10
  159.5 17.2 %copy-start.5 = (f32[256,768]{1,0:T(8,128)}, f32[256,768]{1,0:T(8,128)S(1)}, u32[]{:S(2)}) copy-start(f32[256,768]{1,0:T(8,128)S(1)} %get-tuple-element.915) | copy-start | bytes 2359300
  159.6 17.2 %copy-start.31 = (f32[256]{0:T(256)}, f32[256]{0:T(256)S(1)}, u32[]{:S(2)}) copy-start(f32[256]{0:T(256)S(1)} %broadcast_multiply_fusion) | copy-start | bytes 3076
  161.7 15.0 %copy-start.37 = (f32[256]{0:T(256)}, f32[256]{0:T(256)S(1)}, u32[]{:S(2)}) copy-start(f32[256]{0:T(256)S(1)} %get-tuple-element.947) | copy-start | bytes 3076
  161.7 3.9 copy-start.19
  161.7 3.9 copy-start.22
  161.7 9.1 %slice-start.2 = ((s8[4718592]{0:T(1024)(128)(4,1)}), s8[4194304]{0:T(1024)(128)(4,1)S(1)}, s32[]{:S(2)}) async-start(s8[4718592]{0:T(1024)(128)(4,1)} %bitcast.253), calls=%async_computation.2 | async-start | bytes 8388608
  161.8 11.2 %slice-start = ((s8[4718592]{0:T(1024)(128)(4,1)}), s8[4194304]{0:T(1024)(128)(4,1)S(1)}, s32[]{:S(2)}) async-start(s8[4718592]{0:T(1024)(128)(4,1)} %bitcast.239), calls=%async_computation | async-start | bytes 8388608
  165.7 5.1 slice-start.3
  165.7 7.3 %slice-start.1 = ((s8[4718592]{0:T(1024)(128)(4,1)}), s8[524288]{0:T(1024)(128)(4,1)S(1)}, s32[]{:S(2)}) async-start(s8[4718592]{0:T(1024)(128)(4,1)} %bitcast.239), calls=%async_computation.1 | async-start | bytes 1048576
  170.8 2.2 copy-start.47
  177.1 4.3 copy-start.6
  183.9 2.9 copy-start.34
  183.9 4.3 copy-start.14
  183.9 4.3 copy-start.35
  192.7 2.2 copy-start.1
  196.6 244.9 %copy-start.20 = (f32[768]{0:T(1024)S(1)}, f32[768]{0:T(1024)}, u32[]{:S(2)}) copy-start(f32[768]{0:T(1024)} %param.30) | copy-start | bytes 9220
  196.6 244.9 %copy-start.23 = (f32[768]{0:T(1024)S(1)}, f32[768]{0:T(1024)}, u32[]{:S(2)}) copy-start(f32[768]{0:T(1024)} %param.31) | copy-start | bytes 9220
  196.6 244.9 %copy-start.32 = (f32[256]{0:T(256)S(1)}, f32[256]{0:T(256)}, u32[]{:S(2)}) copy-start(f32[256]{0:T(256)} %copy-done.31) | copy-start | bytes 3076
  196.7 25.1 %collective-permute-start.1 = (bf16[256,1536]{0,1:T(8,128)(2,1)}, bf16[256,1536]{0,1:T(8,128)(2,1)}, u32[]{:S(2)}, u32[]{:S(2)}) collective-permute-start(bf16[256,1536]{0,1:T(8,128)(2,1)} %get-tuple-element.1169), channel_id=1, source_target_pairs={{0,1},{1,2},{2,3},{3,4},{4,5},{5,6},{6,7},{8,9},{9,10},{10,11},{11... | collective-permute-start | bytes 2359304 | tf_op jit(solution)/shard_map/while/body/eval_jaxpr/ppermute | solution.py:22
  219.5 45.2 %collective-permute-start.2 = (bf16[256,1536]{0,1:T(8,128)(2,1)}, bf16[256,1536]{0,1:T(8,128)(2,1)}, u32[]{:S(2)}, u32[]{:S(2)}) collective-permute-start(bf16[256,1536]{0,1:T(8,128)(2,1)} %get-tuple-element.1170), channel_id=1, source_target_pairs={{0,1},{1,2},{2,3},{3,4},{4,5},{5,6},{6,7},{7,0},{8,9},{9,10},{10,1... | collective-permute-start | bytes 2359304 | tf_op jit(solution)/shard_map/while/body/eval_jaxpr/ppermute | solution.py:27
  267.0 3.5 collective-permute-start.1
  269.2 17.2 %collective-permute-start.2 = (bf16[256,1536]{0,1:T(8,128)(2,1)}, bf16[256,1536]{0,1:T(8,128)(2,1)}, u32[]{:S(2)}, u32[]{:S(2)}) collective-permute-start(bf16[256,1536]{0,1:T(8,128)(2,1)} %get-tuple-element.1170), channel_id=1, source_target_pairs={{0,1},{1,2},{2,3},{3,4},{4,5},{5,6},{6,7},{7,0},{8,9},{9,10},{10,1... | collective-permute-start | bytes 2359304 | tf_op jit(solution)/shard_map/while/body/eval_jaxpr/ppermute | solution.py:27
  288.7 7.4 %collective-permute-start.1 = (bf16[256,1536]{0,1:T(8,128)(2,1)}, bf16[256,1536]{0,1:T(8,128)(2,1)}, u32[]{:S(2)}, u32[]{:S(2)}) collective-permute-start(bf16[256,1536]{0,1:T(8,128)(2,1)} %get-tuple-element.1169), channel_id=1, source_target_pairs={{0,1},{1,2},{2,3},{3,4},{4,5},{5,6},{6,7},{8,9},{9,10},{10,11},{11... | collective-permute-start | bytes 2359304 | tf_op jit(solution)/shard_map/while/body/eval_jaxpr/ppermute | solution.py:22
  290.9 24.9 %collective-permute-start.2 = (bf16[256,1536]{0,1:T(8,128)(2,1)}, bf16[256,1536]{0,1:T(8,128)(2,1)}, u32[]{:S(2)}, u32[]{:S(2)}) collective-permute-start(bf16[256,1536]{0,1:T(8,128)(2,1)} %get-tuple-element.1170), channel_id=1, source_target_pairs={{0,1},{1,2},{2,3},{3,4},{4,5},{5,6},{6,7},{7,0},{8,9},{9,10},{10,1... | collective-permute-start | bytes 2359304 | tf_op jit(solution)/shard_map/while/body/eval_jaxpr/ppermute | solution.py:27
  318.1 3.5 collective-permute-start.1
  320.3 26.3 %collective-permute-start.2 = (bf16[256,1536]{0,1:T(8,128)(2,1)}, bf16[256,1536]{0,1:T(8,128)(2,1)}, u32[]{:S(2)}, u32[]{:S(2)}) collective-permute-start(bf16[256,1536]{0,1:T(8,128)(2,1)} %get-tuple-element.1170), channel_id=1, source_target_pairs={{0,1},{1,2},{2,3},{3,4},{4,5},{5,6},{6,7},{7,0},{8,9},{9,10},{10,1... | collective-permute-start | bytes 2359304 | tf_op jit(solution)/shard_map/while/body/eval_jaxpr/ppermute | solution.py:27
  348.9 3.5 collective-permute-start.1
  351.1 26.3 %collective-permute-start.2 = (bf16[256,1536]{0,1:T(8,128)(2,1)}, bf16[256,1536]{0,1:T(8,128)(2,1)}, u32[]{:S(2)}, u32[]{:S(2)}) collective-permute-start(bf16[256,1536]{0,1:T(8,128)(2,1)} %get-tuple-element.1170), channel_id=1, source_target_pairs={{0,1},{1,2},{2,3},{3,4},{4,5},{5,6},{6,7},{7,0},{8,9},{9,10},{10,1... | collective-permute-start | bytes 2359304 | tf_op jit(solution)/shard_map/while/body/eval_jaxpr/ppermute | solution.py:27
  379.6 3.5 collective-permute-start.1
  381.9 26.3 %collective-permute-start.2 = (bf16[256,1536]{0,1:T(8,128)(2,1)}, bf16[256,1536]{0,1:T(8,128)(2,1)}, u32[]{:S(2)}, u32[]{:S(2)}) collective-permute-start(bf16[256,1536]{0,1:T(8,128)(2,1)} %get-tuple-element.1170), channel_id=1, source_target_pairs={{0,1},{1,2},{2,3},{3,4},{4,5},{5,6},{6,7},{7,0},{8,9},{9,10},{10,1... | collective-permute-start | bytes 2359304 | tf_op jit(solution)/shard_map/while/body/eval_jaxpr/ppermute | solution.py:27
  410.4 3.5 collective-permute-start.1
  412.6 26.3 %collective-permute-start.2 = (bf16[256,1536]{0,1:T(8,128)(2,1)}, bf16[256,1536]{0,1:T(8,128)(2,1)}, u32[]{:S(2)}, u32[]{:S(2)}) collective-permute-start(bf16[256,1536]{0,1:T(8,128)(2,1)} %get-tuple-element.1170), channel_id=1, source_target_pairs={{0,1},{1,2},{2,3},{3,4},{4,5},{5,6},{6,7},{7,0},{8,9},{9,10},{10,1... | collective-permute-start | bytes 2359304 | tf_op jit(solution)/shard_map/while/body/eval_jaxpr/ppermute | solution.py:27
  441.2 11.5 %copy-start.45 = (f32[768]{0:T(1024)S(1)}, f32[768]{0:T(1024)}, u32[]{:S(2)}) copy-start(f32[768]{0:T(1024)} %get-tuple-element.858) | copy-start | bytes 9220
  441.2 27.4 %collective-permute-start.3 = (bf16[256,1536]{0,1:T(8,128)(2,1)}, bf16[256,1536]{0,1:T(8,128)(2,1)}, u32[]{:S(2)}, u32[]{:S(2)}) collective-permute-start(bf16[256,1536]{0,1:T(8,128)(2,1)} %get-tuple-element.676), channel_id=1, source_target_pairs={{0,1},{1,2},{2,3},{3,4},{4,5},{5,6},{6,7},{7,0},{8,9},{9,10},{10,1... | collective-permute-start | bytes 2359304 | tf_op jit(solution)/shard_map/ppermute | solution.py:27
  455.9 12.7 %copy-start.3 = (bf16[256,768]{1,0:T(8,128)(2,1)S(1)}, bf16[256,768]{1,0:T(8,128)(2,1)}, u32[]{:S(2)}) copy-start(bf16[256,768]{1,0:T(8,128)(2,1)} %param.23) | copy-start | bytes 1179652
  455.9 12.7 %copy-start.12 = (bf16[256,12,64]{0,2,1:T(8,128)(2,1)S(1)}, bf16[256,12,64]{0,2,1:T(8,128)(2,1)}, u32[]{:S(2)}) copy-start(bf16[256,12,64]{0,2,1:T(8,128)(2,1)} %convert.5) | copy-start | bytes 1179652
  455.9 12.7 %copy-start.18 = (f32[768]{0:T(1024)S(1)}, f32[768]{0:T(1024)}, u32[]{:S(2)}) copy-start(f32[768]{0:T(1024)} %param.26) | copy-start | bytes 9220
  455.9 12.7 %copy-start.27 = (f32[256]{0:T(256)S(1)}, f32[256]{0:T(256)}, u32[]{:S(2)}) copy-start(f32[256]{0:T(256)} %copy-done.26) | copy-start | bytes 3076
  468.6 2.4 copy-start.43
  468.7 2.5 copy-start.29
  468.7 6.1 copy-start.24
  471.1 1.7 copy-start.38
  479.2 118.1 %copy-start.44 = (f32[256]{0:T(256)S(1)}, f32[256]{0:T(256)}, u32[]{:S(2)}) copy-start(f32[256]{0:T(256)} %get-tuple-element.853) | copy-start | bytes 3076
  479.2 118.1 %copy-start.4 = (bf16[256,768]{1,0:T(8,128)(2,1)S(1)}, bf16[256,768]{1,0:T(8,128)(2,1)}, u32[]{:S(2)}) copy-start(bf16[256,768]{1,0:T(8,128)(2,1)} %param.23) | copy-start | bytes 1179652
  479.2 118.1 %copy-start.30 = (f32[256]{0:T(256)S(1)}, f32[256]{0:T(256)}, u32[]{:S(2)}) copy-start(f32[256]{0:T(256)} %copy-done.28) | copy-start | bytes 3076
  479.2 118.1 %copy-start.39 = (f32[256]{0:T(256)S(1)}, f32[256]{0:T(256)}, u32[]{:S(2)}) copy-start(f32[256]{0:T(256)} %copy-done.38) | copy-start | bytes 3076
  479.3 118.1 %copy-start.41 = (f32[256]{0:T(256)S(1)}, f32[256]{0:T(256)}, u32[]{:S(2)}) copy-start(f32[256]{0:T(256)} %copy-done.40) | copy-start | bytes 3076
  595.1 10.7 %copy-start.21 = (f32[24,768]{1,0:T(8,128)S(1)}, f32[24,768]{1,0:T(8,128)}, u32[]{:S(2)}) copy-start(f32[24,768]{1,0:T(8,128)} %get-tuple-element.1218) | copy-start | bytes 221188
  595.1 11.3 %copy-start.17 = (f32[24,3072]{1,0:T(8,128)S(1)}, f32[24,3072]{1,0:T(8,128)}, u32[]{:S(2)}) copy-start(f32[24,3072]{1,0:T(8,128)} %get-tuple-element.1221) | copy-start | bytes 884740
  595.1 12.0 %copy-start.16 = (f32[96,768]{1,0:T(8,128)S(1)}, f32[96,768]{1,0:T(8,128)}, u32[]{:S(2)}) copy-start(f32[96,768]{1,0:T(8,128)} %get-tuple-element.1222) | copy-start | bytes 884740
  (7 other events, 7.1 us)

commit v2 on v0

--- a/solution.py
+++ b/solution.py
@@ -1,11 +1,16 @@
+import functools
+
 import jax
 import jax.numpy as jnp
 from jax import lax
+from jax.experimental import pallas as pl
+from jax.experimental.pallas import tpu as pltpu
 from jax.sharding import PartitionSpec as P
 
 D = 768
 HEADS = 12
 HEAD_DIM = 64
+MESH = pl.DeviceIdType.MESH
 
 
 epsilon = 1e-05
@@ -272,6 +277,640 @@
     )
 
 
+def rows_of(start, count):
+    return pl.ds(pl.multiple_of(start, 16), count)
+
+
+def matmul(left, right):
+    return jnp.dot(left, right, preferred_element_type=jnp.float32)
+
+
+def signed_terms(scores):
+    square = scores * scores + 1.0
+    inverse = lax.rsqrt(square)
+    return inverse, scores * inverse, jnp.exp(square * inverse)
+
+
+def valid_columns(span, start, count):
+    pos = start + lax.broadcasted_iota(jnp.int32, (1, count), 1)
+    return (pos >= span[0, 0]) & (pos < span[0, 1])
+
+
+def greet(partners):
+    barrier = pltpu.get_barrier_semaphore()
+    for partner in partners:
+        pl.semaphore_signal(barrier, inc=1, device_id=partner, device_id_type=MESH)
+    pl.semaphore_wait(barrier, len(partners))
+
+
+def sender(send_sems, recv_sems):
+    count = [0]
+
+    def send(src, dst, target):
+        slot = count[0]
+        count[0] += 1
+        copy = pltpu.make_async_remote_copy(
+            src_ref=src, dst_ref=dst, send_sem=send_sems.at[slot], recv_sem=recv_sems.at[slot],
+            device_id=target, device_id_type=MESH,
+        )
+        copy.start()
+        return copy
+
+    return send
+
+
+def place():
+    grp, seq = lax.axis_index("grp"), lax.axis_index("seq")
+    zed, core = seq // 2, seq % 2
+    sibling = (grp, zed * 2 + 1 - core)
+    along = [(zed + k) % 4 for k in range(4)]
+    return grp, seq, zed, core, sibling, along
+
+
+def attend_kernel(
+    proj, span, mixed_out, q_all, kv_all, mix_all, tot_all,
+    masked, arrived, leaving, own, keys, send_sems, recv_sems,
+):
+    tokens = proj.shape[-1]
+    f32, bf16 = jnp.float32, jnp.bfloat16
+    grp, seq, zed, core, sibling, along = place()
+    line = [(grp, along[k] * 2 + core) for k in (1, 2, 3)]
+    valid_here = valid_columns(span, seq * tokens, tokens)
+    keep = valid_here.astype(f32)
+
+    def mask_head(head, _):
+        for part in range(3):
+            masked[part, head] = (proj[part, head].astype(f32) * keep).astype(bf16)
+        return 0
+
+    lax.fori_loop(0, HEADS, mask_head, 0)
+    greet([sibling] + line)
+    send = sender(send_sems, recv_sems)
+    going = []
+    for h in range(3):
+        for k in (1, 2, 3):
+            head = along[k] * 3 + h
+            going.append(send(masked.at[0, head], q_all.at[h, zed], line[k - 1]))
+            going.append(
+                send(masked.at[pl.ds(1, 2), head], kv_all.at[h, zed, core], line[k - 1])
+            )
+    for h in range(3):
+        head = zed * 3 + h
+        q_all[h, zed] = masked[0, head]
+        for part in range(2):
+            kv_all[h, zed, core, part] = masked[1 + part, head]
+
+    def alone(head, _):
+        q, k, v = (proj[part, head].astype(f32) for part in range(3))
+        _, signed, terms = signed_terms(jnp.sum(q * k, axis=0, keepdims=True))
+        weight = (signed * terms).astype(bf16).astype(f32)
+        own[head] = (weight * v / terms).astype(bf16)
+        return 0
+
+    lax.fori_loop(0, HEADS, alone, 0)
+    extra = span[0, 0].astype(f32) * signed_terms(jnp.zeros((1, tokens), f32))[2]
+
+    returning = []
+    for h in range(3):
+        for copy in going[h * 6 : h * 6 + 6]:
+            copy.wait_recv()
+        relay = send(kv_all.at[h, :, core], kv_all.at[h, :, core], sibling)
+
+        def turn(side):
+            def one(z, _):
+                keys[z, rows_of(side * tokens, tokens), :] = kv_all[h, z, side, 0].T
+                return 0
+
+            lax.fori_loop(0, 4, one, 0)
+
+        turn(core)
+        relay.wait()
+        turn(1 - core)
+
+        def query_block(z, _):
+            queries = q_all[h, z]
+
+            def pair(other, carry, last=False):
+                total, mixed = carry
+                for side in range(2):
+                    scores = matmul(keys[other, pl.ds(side * tokens, tokens), :], queries)
+                    _, signed, terms = signed_terms(scores)
+                    if last:
+                        key_pos = lax.broadcasted_iota(jnp.int32, scores.shape, 0)
+                        query_pos = lax.broadcasted_iota(jnp.int32, scores.shape, 1)
+                        seen = key_pos + side * tokens <= query_pos + core * tokens
+                        terms = jnp.where(seen, terms, 0.0)
+                    total = total + jnp.sum(terms.reshape(tokens // 8, 8, tokens), axis=0)
+                    weights = (signed * terms).astype(bf16)
+                    mixed = mixed + matmul(kv_all[h, other, side, 1], weights)
+                return total, mixed
+
+            zero = (jnp.zeros((8, tokens), f32), jnp.zeros((HEAD_DIM, tokens), f32))
+            total, mixed = pair(z, lax.fori_loop(0, z, pair, zero), True)
+            total = jnp.sum(total, axis=0, keepdims=True) - extra
+            fine = valid_columns(span, (2 * z + core) * tokens, tokens)
+            total = jnp.where(fine, total, 1.0)
+            mixed = mixed / total
+            mix_all[h, z] = mixed
+            tot_all[h, z] = total
+            leaving[h, z] = mixed.astype(bf16)
+            return 0
+
+        lax.fori_loop(0, 4, query_block, 0)
+        for k in (1, 2, 3):
+            returning.append(
+                send(leaving.at[h, along[k]], arrived.at[zed * 3 + h], line[k - 1])
+            )
+        arrived[zed * 3 + h] = leaving[h, zed]
+    for copy in returning:
+        copy.wait_recv()
+
+    def join(head, _):
+        mixed_out[head] = jnp.where(
+            valid_here, arrived[head].astype(f32), own[head].astype(f32)
+        ).astype(bf16)
+        return 0
+
+    lax.fori_loop(0, HEADS, join, 0)
+    for copy in going + returning:
+        copy.wait_send()
+
+
+def attend(proj, span):
+    f32, bf16 = jnp.float32, jnp.bfloat16
+    tokens = proj.shape[-1]
+    vmem, smem = pl.BlockSpec(memory_space=pltpu.VMEM), pl.BlockSpec(memory_space=pltpu.SMEM)
+    block = (HEAD_DIM, tokens)
+    copies = 18 + 3 + 9
+    return pl.pallas_call(
+        attend_kernel,
+        out_shape=[
+            jax.ShapeDtypeStruct((HEADS,) + block, bf16),
+            jax.ShapeDtypeStruct((3, 4) + block, bf16),
+            jax.ShapeDtypeStruct((3, 4, 2, 2) + block, bf16),
+            jax.ShapeDtypeStruct((3, 4) + block, f32),
+            jax.ShapeDtypeStruct((3, 4, 1, tokens), f32),
+        ],
+        in_specs=[vmem, smem],
+        out_specs=[vmem] * 5,
+        scratch_shapes=[
+            pltpu.VMEM((3, HEADS) + block, bf16),
+            pltpu.VMEM((HEADS,) + block, bf16),
+            pltpu.VMEM((3, 4) + block, bf16),
+            pltpu.VMEM((HEADS,) + block, bf16),
+            pltpu.VMEM((4, 2 * tokens, HEAD_DIM), bf16),
+            pltpu.SemaphoreType.DMA((copies,)),
+            pltpu.SemaphoreType.DMA((copies,)),
+        ],
+        compiler_params=pltpu.CompilerParams(
+            collective_id=1, has_side_effects=True, vmem_limit_bytes=48 * 2**20
+        ),
+    )(proj, span)
+
+
+def add_halves(term, first, column, base, count):
+    def add(i, _):
+        at = rows_of(base + i * 16, 16)
+        first[at, :] = (
+            term[at, column].astype(jnp.float32) + first[at, :].astype(jnp.float32)
+        ).astype(jnp.bfloat16)
+        return 0
+
+    lax.fori_loop(0, count // 16, add, 0)
+
+
+def add_groups(term, first, second, held, column, base, count):
+    def add(i, _):
+        at, here = rows_of(base + i * 16, 16), rows_of(i * 16, 16)
+        total = term[at, column].astype(jnp.float32) + first[at, :].astype(jnp.float32)
+        for j in range(3):
+            total = total + second[j, here, :].astype(jnp.float32)
+        held[here, :] = total.astype(jnp.bfloat16)
+        return 0
+
+    lax.fori_loop(0, count // 16, add, 0)
+
+
+def across_groups(grp):
+    return [((grp // 2 + k // 2) % 2) * 2 + (grp % 2 + k % 2) % 2 for k in range(4)]
+
+
+def send_halves(send, term, first, core, across, sibling):
+    rows, columns = term.shape[0] // 4, term.shape[1] // 2
+    away = pl.ds(pl.multiple_of((1 - core) * columns, 128), columns)
+    copies = {}
+    for k in (1, 2, 3, 0):
+        at = rows_of(across[k] * rows, rows)
+        copies[k] = send(term.at[at, away], first.at[at, :], sibling)
+    return copies
+
+
+def send_quarters(send, copies, term, first, second, core, across, seq):
+    rows, columns = term.shape[0] // 4, term.shape[1] // 2
+    column = pl.ds(pl.multiple_of(core * columns, 128), columns)
+    going = []
+    for k in (1, 2, 3):
+        base = across[k] * rows
+        copies[k].wait_recv()
+        add_halves(term, first, column, base, rows)
+        going.append(send(first.at[rows_of(base, rows), :], second.at[k - 1], (across[k], seq)))
+    return going
+
+
+def sum_quarters(copies, going, term, first, second, held, core, across):
+    rows, columns = term.shape[0] // 4, term.shape[1] // 2
+    column = pl.ds(pl.multiple_of(core * columns, 128), columns)
+    copies[0].wait_recv()
+    for copy in going:
+        copy.wait_recv()
+    add_groups(term, first, second, held, column, across[0] * rows, rows)
+
+
+def attend_back_kernel(many, *refs):
+    gmix, proj, q_all, kv_all, mix_all, tot_all, span = refs[:7]
+    terms_in = refs[7 : 7 + many]
+    grad_out = refs[7 + many]
+    held = refs[8 + many : 8 + 2 * many]
+    rest = refs[8 + 2 * many :]
+    first, second = rest[:many], rest[many : 2 * many]
+    (gm_in, own, keys, values, g_all, gt_all, grad_kv, part_out, part_in, leaving, arrived,
+     send_sems, recv_sems) = rest[2 * many :]
+    tokens = proj.shape[-1]
+    f32, bf16 = jnp.float32, jnp.bfloat16
+    grp, seq, zed, core, sibling, along = place()
+    line = [(grp, along[k] * 2 + core) for k in (1, 2, 3)]
+    across = across_groups(grp)
+    valid_here = valid_columns(span, seq * tokens, tokens)
+
+    greet([sibling] + line + [(across[k], seq) for k in (1, 2, 3)])
+    send = sender(send_sems, recv_sems)
+    coming = []
+    for h in range(3):
+        for k in (1, 2, 3):
+            coming.append(send(gmix.at[along[k] * 3 + h], gm_in.at[h, zed], line[k - 1]))
+    halves = [send_halves(send, terms_in[a], first[a], core, across, sibling) for a in range(many)]
+    for h in range(3):
+        gm_in[h, zed] = gmix[zed * 3 + h]
+
+    def alone(head, _):
+        q, k, v = (proj[part, head].astype(f32) for part in range(3))
+        g = gmix[head].astype(f32)
+        inverse, signed, terms = signed_terms(jnp.sum(q * k, axis=0, keepdims=True))
+        weight = (signed * terms).astype(bf16).astype(f32)
+        total = 1.0 / terms
+        grad_total = -jnp.sum(g * (weight * v), axis=0, keepdims=True) * total * total
+        g = (g * total).astype(bf16).astype(f32)
+        grad_weight = jnp.sum(g * v, axis=0, keepdims=True)
+        square = inverse * inverse
+        grad_score = terms * (grad_weight * (1.0 + square * (inverse - 1.0)) + grad_total * signed)
+        grad_score = grad_score.astype(bf16).astype(f32)
+        own[0, head] = (grad_score * k * 0.125).astype(bf16)
+        own[1, head] = (grad_score * q).astype(bf16)
+        own[2, head] = (weight * g).astype(bf16)
+        return 0
+
+    lax.fori_loop(0, HEADS, alone, 0)
+
+    def turn(i, _):
+        h, z = i // 4, i % 4
+        for side in range(2):
+            at = pl.ds(side * tokens, tokens)
+            keys[h, z, at, :] = kv_all[h, z, side, 0].T
+            values[h, z, at, :] = kv_all[h, z, side, 1].T
+        return 0
+
+    lax.fori_loop(0, 12, turn, 0)
+    quarters = [
+        send_quarters(send, halves[a], terms_in[a], first[a], second[a], core, across, seq)
+        for a in range(many)
+    ]
+
+    swaps, sends = [], []
+
+    def finish(h):
+        swaps[h].wait_recv()
+
+        def merge(z, _):
+            for part in range(2):
+                total = grad_kv[h, z, core, part] + part_in[h, z, part].astype(f32)
+                leaving[h, z, 1 + part] = total.astype(bf16)
+            return 0
+
+        lax.fori_loop(0, 4, merge, 0)
+        for k in (1, 2, 3):
+            sends.append(send(leaving.at[h, along[k]], arrived.at[zed * 3 + h], line[k - 1]))
+        arrived[zed * 3 + h] = leaving[h, zed]
+
+    for h in range(3):
+        for copy in coming[h * 3 : h * 3 + 3]:
+            copy.wait_recv()
+
+        def prepare(z, _):
+            g = gm_in[h, z].astype(f32)
+            total = 1.0 / tot_all[h, z]
+            g_all[z] = (g * total).astype(bf16)
+            gt_all[z] = -jnp.sum(g * mix_all[h, z], axis=0, keepdims=True) * total
+            for side in range(2):
+                for part in range(2):
+                    grad_kv[h, z, side, part] = jnp.zeros((HEAD_DIM, tokens), f32)
+            return 0
+
+        lax.fori_loop(0, 4, prepare, 0)
+
+        def query_block(z, _):
+            queries, grads, grad_total = q_all[h, z], g_all[z], gt_all[z]
+
+            def pair(other, grad_query, last=False):
+                for side in range(2):
+                    at = pl.ds(side * tokens, tokens)
+                    scores = matmul(keys[h, other, at, :], queries)
+                    grad_weights = matmul(values[h, other, at, :], grads)
+                    inverse, signed, terms = signed_terms(scores)
+                    if last:
+                        key_pos = lax.broadcasted_iota(jnp.int32, scores.shape, 0)
+                        query_pos = lax.broadcasted_iota(jnp.int32, scores.shape, 1)
+                        seen = key_pos + side * tokens <= query_pos + core * tokens
+                        terms = jnp.where(seen, terms, 0.0)
+                    weights = (signed * terms).astype(bf16)
+                    slope = 1.0 + (inverse * inverse) * (inverse - 1.0)
+                    grad_scores = terms * (grad_weights * slope + grad_total * signed)
+                    grad_scores = grad_scores.astype(bf16)
+                    grad_query = grad_query + matmul(kv_all[h, other, side, 0], grad_scores)
+                    grad_kv[h, other, side, 0] += contract_cols(queries, grad_scores)
+                    grad_kv[h, other, side, 1] += contract_cols(grads, weights)
+                return grad_query
+
+            zero = jnp.zeros((HEAD_DIM, tokens), f32)
+            grad_query = pair(z, lax.fori_loop(0, z, pair, zero), True)
+            leaving[h, z, 0] = (grad_query * 0.125).astype(bf16)
+            return 0
+
+        lax.fori_loop(0, 4, query_block, 0)
+
+        def pack(z, _):
+            for part in range(2):
+                part_out[h, z, part] = grad_kv[h, z, 1 - core, part].astype(bf16)
+            return 0
+
+        lax.fori_loop(0, 4, pack, 0)
+        swaps.append(send(part_out.at[h], part_in.at[h], sibling))
+        if h > 0:
+            finish(h - 1)
+    finish(2)
+    for a in range(many):
+        sum_quarters(
+            halves[a], quarters[a], terms_in[a], first[a], second[a], held[a], core, across
+        )
+    for copy in sends:
+        copy.wait_recv()
+
+    def join(head, _):
+        for part in range(3):
+            grad_out[part, head] = jnp.where(
+                valid_here, arrived[head, part].astype(f32), own[part, head].astype(f32)
+            ).astype(bf16)
+        return 0
+
+    lax.fori_loop(0, HEADS, join, 0)
+    for copy in coming + swaps + sends:
+        copy.wait_send()
+    for a in range(many):
+        for copy in list(halves[a].values()) + quarters[a]:
+            copy.wait_send()
+
+
+def attend_back(gmix, proj, saved, span, terms):
+    f32, bf16 = jnp.float32, jnp.bfloat16
+    tokens = proj.shape[-1]
+    many = len(terms)
+    vmem, smem = pl.BlockSpec(memory_space=pltpu.VMEM), pl.BlockSpec(memory_space=pltpu.SMEM)
+    block = (HEAD_DIM, tokens)
+    copies = 9 + 7 * many + 3 + 9
+    shapes = [t.shape for t in terms]
+    return pl.pallas_call(
+        functools.partial(attend_back_kernel, many),
+        out_shape=[jax.ShapeDtypeStruct((3, HEADS) + block, bf16)]
+        + [jax.ShapeDtypeStruct((r // 4, c // 2), bf16) for r, c in shapes],
+        in_specs=[vmem] * 6 + [smem] + [vmem] * many,
+        out_specs=[vmem] * (1 + many),
+        scratch_shapes=[pltpu.VMEM((r, c // 2), bf16) for r, c in shapes]
+        + [pltpu.VMEM((3, r // 4, c // 2), bf16) for r, c in shapes]
+        + [
+            pltpu.VMEM((3, 4) + block, bf16),
+            pltpu.VMEM((3, HEADS) + block, bf16),
+            pltpu.VMEM((3, 4, 2 * tokens, HEAD_DIM), bf16),
+            pltpu.VMEM((3, 4, 2 * tokens, HEAD_DIM), bf16),
+            pltpu.VMEM((4,) + block, bf16),
+            pltpu.VMEM((4, 1, tokens), f32),
+            pltpu.VMEM((3, 4, 2, 2) + block, f32),
+            pltpu.VMEM((3, 4, 2) + block, bf16),
+            pltpu.VMEM((3, 4, 2) + block, bf16),
+            pltpu.VMEM((3, 4, 3) + block, bf16),
+            pltpu.VMEM((HEADS, 3) + block, bf16),
+            pltpu.SemaphoreType.DMA((copies,)),
+            pltpu.SemaphoreType.DMA((copies,)),
+        ],
+        compiler_params=pltpu.CompilerParams(
+            collective_id=2, has_side_effects=True, vmem_limit_bytes=60 * 2**20
+        ),
+    )(gmix, proj, *saved, span, *terms)
+
+
+def send_line(send, held, third, along, line):
+    rows = held.shape[0] // 4
+    return [
+        send(held.at[rows_of(along[k] * rows, rows), :], third.at[k - 1], line[k - 1])
+        for k in (1, 2, 3)
+    ]
+
+
+def sum_line(send, copies, held, third, mine, out, zed, core, sibling):
+    rows, columns = held.shape[0] // 4, held.shape[1]
+    for copy in copies:
+        copy.wait_recv()
+    total = held[rows_of(zed * rows, rows), :].astype(jnp.float32)
+    for j in range(3):
+        total = total + third[j].astype(jnp.float32)
+    mine[...] = total
+    column = pl.ds(pl.multiple_of(core * columns, 128), columns)
+    half = rows // 2
+    away = pl.ds(pl.multiple_of((1 - core) * half, 8), half)
+    out[:, column] = mine[pl.ds(pl.multiple_of(core * half, 8), half), :]
+    return send(mine.at[away, :], out.at[:, column], sibling)
+
+
+def finish_kernel(many, *refs):
+    term, small_in = refs[:2]
+    early = refs[2 : 2 + many]
+    outs = refs[2 + many : 3 + 2 * many]
+    small_out = refs[3 + 2 * many]
+    rest = refs[4 + 2 * many :]
+    third, mine = rest[: many + 1], rest[many + 1 : 2 * many + 2]
+    first, second, held, small_a, small_b, small_c, send_sems, recv_sems = rest[2 * many + 2 :]
+    grp, seq, zed, core, sibling, along = place()
+    line = [(grp, along[k] * 2 + core) for k in (1, 2, 3)]
+    across = across_groups(grp)
+    greet([sibling] + line + [(across[k], seq) for k in (1, 2, 3)])
+    send = sender(send_sems, recv_sems)
+    swap = send(small_in, small_a.at[1], sibling)
+    halves = send_halves(send, term, first, core, across, sibling)
+    lines = [send_line(send, early[a], third[1 + a], along, line) for a in range(many)]
+    swap.wait_recv()
+    small_a[0] = small_in[...] + small_a[1]
+    small_b[pl.ds(grp, 1)] = small_a[0:1]
+    planes = [send(small_a.at[0], small_b.at[grp], (across[k], seq)) for k in (1, 2, 3)]
+    quarters = send_quarters(send, halves, term, first, second, core, across, seq)
+    for copy in planes:
+        copy.wait_recv()
+    small_c[pl.ds(zed, 1)] = (small_b[0:1] + small_b[1:2]) + (small_b[2:3] + small_b[3:4])
+    columns = [send(small_c.at[zed], small_c.at[zed], line[k - 1]) for k in (1, 2, 3)]
+    swaps = []
+    for a in range(many):
+        swaps.append(
+            sum_line(
+                send, lines[a], early[a], third[1 + a], mine[1 + a], outs[1 + a], zed, core, sibling
+            )
+        )
+    for copy in columns:
+        copy.wait_recv()
+    small_out[...] = (small_c[0] + small_c[1]) + (small_c[2] + small_c[3])
+    sum_quarters(halves, quarters, term, first, second, held, core, across)
+    last = send_line(send, held, third[0], along, line)
+    swaps.append(sum_line(send, last, held, third[0], mine[0], outs[0], zed, core, sibling))
+    for copy in swaps:
+        copy.wait_recv()
+    for copy in [swap] + planes + columns + swaps + quarters + last + list(halves.values()):
+        copy.wait_send()
+    for copies in lines:
+        for copy in copies:
+            copy.wait_send()
+
+
+def finish(term, small, early):
+    f32, bf16 = jnp.float32, jnp.bfloat16
+    many = len(early)
+    vmem = pl.BlockSpec(memory_space=pltpu.VMEM)
+    r, c = term.shape
+    helds = [(r // 4, c // 2)] + [e.shape for e in early]
+    copies = 1 + 4 + 3 * many + 3 + 3 + 3 + many + 3 + 1
+    return pl.pallas_call(
+        functools.partial(finish_kernel, many),
+        out_shape=[jax.ShapeDtypeStruct((hr // 8, 2 * hc), f32) for hr, hc in helds]
+        + [jax.ShapeDtypeStruct(small.shape, f32)],
+        in_specs=[vmem] * (2 + many),
+        out_specs=[vmem] * (2 + many),
+        scratch_shapes=[pltpu.VMEM((3, hr // 4, hc), bf16) for hr, hc in helds]
+        + [pltpu.VMEM((hr // 4, hc), f32) for hr, hc in helds]
+        + [
+            pltpu.VMEM((r, c // 2), bf16),
+            pltpu.VMEM((3, r // 4, c // 2), bf16),
+            pltpu.VMEM((r // 4, c // 2), bf16),
+            pltpu.VMEM((2,) + small.shape, f32),
+            pltpu.VMEM((4,) + small.shape, f32),
+            pltpu.VMEM((4,) + small.shape, f32),
+            pltpu.SemaphoreType.DMA((copies,)),
+            pltpu.SemaphoreType.DMA((copies,)),
+        ],
+        compiler_params=pltpu.CompilerParams(
+            collective_id=0, has_side_effects=True, vmem_limit_bytes=48 * 2**20
+        ),
+    )(term, small, *early)
+
+
+def per_device_planned(
+    block_input,
+    out_grad,
+    seq_span,
+    ln1_gain,
+    ln1_bias,
+    w_qkv,
+    w_out,
+    ln2_gain,
+    ln2_bias,
+    w_up,
+    w_down,
+):
+    f32, bf16 = jnp.float32, jnp.bfloat16
+    tokens, width = block_input.shape
+    seq_count = lax.axis_size("seq")
+    seq_index = lax.axis_index("seq")
+    token_pos = seq_index * tokens + jnp.arange(tokens, dtype=jnp.int32)
+    valid = (token_pos >= seq_span[0, 0]) & (token_pos < seq_span[0, 1])
+    inputs = block_input.astype(f32)
+    normed = layer_norm(inputs, ln1_gain, ln1_bias).astype(bf16)
+    proj = lax.dot_general(w_qkv, normed, (((0,), (1,)), ((), ())), preferred_element_type=f32)
+    scale = jnp.where(jnp.arange(3 * width) < width, 0.125, 1.0).astype(f32)
+    proj = (proj * scale[:, None]).astype(bf16).reshape(3, HEADS, HEAD_DIM, tokens)
+    mixed, *saved = attend(proj, seq_span)
+    mixed = mixed.reshape(width, tokens)
+
+    attn_out = contract_rows(mixed, w_out)
+    middle = inputs + attn_out
+    normed_two = layer_norm(middle, ln2_gain, ln2_bias).astype(bf16)
+    up_proj = jnp.dot(normed_two, w_up, preferred_element_type=f32)
+    activated, gelu_pull = jax.vjp(lambda u: jax.nn.gelu(u, approximate=True), up_proj)
+    activated = activated.astype(bf16)
+    mlp_out = jnp.dot(activated, w_down, preferred_element_type=f32)
+    output = middle + mlp_out
+    valid_rows = valid.astype(f32)[:, None]
+    rms_terms = (
+        jnp.sum(valid_rows * output * output),
+        jnp.sum(valid_rows * attn_out * attn_out),
+        jnp.sum(valid_rows * mlp_out * mlp_out),
+        jnp.sum(valid_rows) * width,
+    )
+    term_down = contract_rows(activated, out_grad).astype(bf16)
+    grad_up = gelu_pull(contract_cols(out_grad, w_down))[0].astype(bf16)
+    term_up = contract_rows(normed_two, grad_up).astype(bf16)
+    grad_norm_two = contract_cols(grad_up, w_up)
+    _, norm_pull_two = jax.vjp(layer_norm, middle, ln2_gain, ln2_bias)
+    grad_mid_norm, grad_gain_two, grad_bias_two = norm_pull_two(grad_norm_two)
+    grad_middle = out_grad.astype(f32) + grad_mid_norm
+    grad_attn = grad_middle.astype(bf16)
+    term_out = jnp.dot(mixed, grad_attn, preferred_element_type=f32).astype(bf16)
+    grad_mixed = contract_cols(w_out, grad_attn).astype(bf16)
+    grad_qkv, *early = attend_back(
+        grad_mixed.reshape(HEADS, HEAD_DIM, tokens),
+        proj,
+        saved,
+        seq_span,
+        (term_down, term_up, term_out),
+    )
+    grad_qkv = grad_qkv.reshape(3 * width, tokens)
+    term_qkv = lax.dot_general(
+        normed, grad_qkv, (((0,), (1,)), ((), ())), preferred_element_type=f32
+    ).astype(bf16)
+    grad_norm_one = lax.dot_general(
+        grad_qkv, w_qkv, (((0,), (1,)), ((), ())), preferred_element_type=f32
+    )
+    _, norm_pull_one = jax.vjp(layer_norm, inputs, ln1_gain, ln1_bias)
+    grad_in_norm, grad_gain_one, grad_bias_one = norm_pull_one(grad_norm_one)
+    input_grad = (grad_middle + grad_in_norm).astype(bf16)
+
+    rms_row = jnp.pad(jnp.stack(rms_terms), (0, width - 4))
+    small = jnp.stack(
+        [grad_gain_one, grad_bias_one, grad_gain_two, grad_bias_two, rms_row] + [rms_row] * 3
+    )
+    sum_qkv, sum_down, sum_up, sum_out, small = finish(term_qkv, small, early)
+    rms_stats = jnp.sqrt(small[4, :3] / small[4, 3])
+    count = width // (seq_count * lax.axis_size("grp"))
+    start = (lax.axis_index("grp") * seq_count + seq_index) * count
+    vecs = [lax.dynamic_slice(small[i], (start,), (count,)) for i in range(4)]
+    return (
+        output.astype(bf16),
+        input_grad,
+        vecs[0],
+        vecs[1],
+        sum_qkv,
+        sum_out,
+        vecs[2],
+        vecs[3],
+        sum_up,
+        sum_down,
+        rms_stats,
+    )
+
+
 def solution(mesh):
     placed = (
         P(("grp", "seq"), None),
@@ -286,8 +925,9 @@
         P(),
         P(),
     )
+    planned = mesh.shape["grp"] == 4 and mesh.shape["seq"] == 8
     return jax.shard_map(
-        per_device,
+        per_device_planned if planned else per_device,
         mesh=mesh,
         in_specs=placed,
         out_specs=(

time: 912 us -> 246 us (0.27)
  waiting for transfers between devices: 534 us -> 0 us
  Pallas kernels: 0 us -> 165 us
  starting transfers between devices: 139 us -> 0 us
  blocking collectives: 42 us -> 0 us
  local copies, waits for them, and re-layouts: 59.9 us -> 19.2 us
  other arithmetic: 39.7 us -> 10.5 us
  between operations: 16 us -> 1.82 us
  matrix products: 60.1 us -> 48.5 us
  loops' own time: 10.8 us -> 0 us
    reduce_scatter x4 -> x0, waiting for transfers between devices: 331 us -> none  [the longest x1 142 us: per_device(): lax.psum_scatter(grad_w_down, ('grp', 'seq'), scatter_dimension=0, tiled=...]
    ppermute x22 -> x0, waiting for transfers between devices: 203 us -> none  [the longest x8 196 us: shifted(): lax.ppermute(array, axis, [(i, (i + by) % devices) for i in range(devices)])]
    pallas_call x0 -> x3, Pallas kernels: none -> 165 us  [the longest x1 72.5 us: attend_back(): pl.pallas_call(functools.partial(attend_back_kernel, many), out_shape=[ja...]
    ppermute x22 -> x0, starting transfers between devices: 139 us -> none  [the longest x14 134 us: passed_along(): return lax.ppermute(array, axis, pairs)]
    unnamed x1 -> x0, blocking collectives: 42 us -> none
    while x14 -> x0, local copies, waits for them, and re-layouts: 28.9 us -> none
    add x10 -> x0, other arithmetic: 16 us -> none  [the longest x7 16 us: backward_hop(): return (moving, grad_acc + new_terms, grad_run)]
    another operation x18 -> x0, loops' own time: 10.8 us -> none  [the longest x1 5.04 us: per_device(): lax.fori_loop(1, seq_count, backward_hop, (kv_pair, local_terms, grad_que...]
  transfers between devices with their start and end apart: 26 -> 0, of which waited for: 22 -> 0; matrix products, arithmetic and copies ran while one was open for 10% -> 0% of each run, Pallas kernels for 0% -> 0%
where the time goes in v2:
time: 246 us; the launch traced here: 245 us
  Pallas kernels  165 us (67%)
  matrix products  48.5 us (20%)
  local copies, waits for them, and re-layouts  19.2 us (8%)
  other arithmetic  10.5 us (4%)
    pallas_call x1, Pallas kernels, attend_back(): pl.pallas_call(functools.partial(attend_back_kernel, many), out_shape=[ja...  72.5 us
    pallas_call x1, Pallas kernels, attend(): pl.pallas_call(attend_kernel, out_shape=[jax.ShapeDtypeStruct((HEADS,) +...  48.8 us
    pallas_call x1, Pallas kernels, finish(): pl.pallas_call(functools.partial(finish_kernel, many), out_shape=[jax.Sha...  43.4 us
    dot_general x3, matrix products, contract_cols(): lax.dot_general(left, right, (((1,), (1,)), ((), ())), preferred_element_...  12.4 us
    dot_general x3, matrix products, contract_rows(): lax.dot_general(left, right, (((0,), (0,)), ((), ())), preferred_element_...  11.9 us
    dot_general x1, matrix products, per_device_planned(): up_proj = jnp.dot(normed_two, w_up, preferred_element_type=f32)  6.98 us
    unnamed x94, local copies, waits for them, and re-layouts  6.95 us
    dot_general x1, matrix products, per_device_planned(): mlp_out = jnp.dot(activated, w_down, preferred_element_type=f32)  5.92 us

profile of v2, /device:TPU:0, one launch (start us, length us, event | category | flops | bytes accessed | tf_op | source)
XLA Modules:
  0.0 244.7 jit_solution(4579847154207710507)
XLA Ops:
  0.6 0.0 copy-start
  0.7 1.3 convert_reduce_fusion
  2.0 1.2 fusion.19
  3.2 1.3 fusion.42
  4.5 0.0 copy-done.41
  4.6 3.2 %fusion.1 = bf16[2304,256]{0,1:T(8,128)(2,1)} fusion(bf16[768,2304]{1,0:T(8,128)(2,1)S(1)} %copy-done, f32[2304]{0:T(1024)S(1)} %fusion.25, bf16[256,768]{1,0:T(8,128)(2,1)} %param.11, f32[768]{0:T(1024)} %param.15, f32[768]{0:T(1024)} %param.14, f32[256]{0:T(256)S(1)} %fusion.26, f32[256]{0:T(256)S(1)} %broadcast_multiply_fusion.1), kind=kOutput, calls=%fused_computation.7 | convolution fusion | flops 908328960 | bytes 5129216 | tf_op jit(solution)/shard_map/dot_general | solution.py:841
  7.8 2.4 copy.22
  10.2 5.7 %fusion.43 = f32[256,3072]{1,0:T(8,128)} fusion(bf16[256,768]{1,0:T(8,128)(2,1)} %param.12, bf16[3072,768]{1,0:T(8,128)(2,1)} %param.21), kind=kOutput, calls=%fused_computation.84 | convolution fusion | flops 1207959552 | bytes 8257536 | tf_op jit(solution)/shard_map/dot_general | solution.py:44
  15.8 0.0 copy-start.29
  15.9 48.8 %shard_map.194 = (bf16[12,64,256]{2,1,0:T(8,128)(2,1)S(1)}, bf16[3,4,64,256]{3,2,1,0:T(8,128)(2,1)S(1)}, bf16[3,4,2,2,64,256]{5,4,3,2,1,0:T(8,128)(2,1)S(1)}, f3...) custom-call(bf16[3,12,64,256]{3,2,1,0:T(8,128)(2,1)S(1)} %bitcast.44, s32[1,2]{1,0:T(1,128)S(1)} %copy-done.11), custom_call_target="tpu_custom_call" | custom-call | tf_op jit(solution)/shard_map/pallas_call | solution.py:445
  64.6 0.0 copy-start.2
  64.7 1.1 copy-done.2
  65.8 0.7 copy-done.3
  66.5 1.4 fusion.40
  68.0 0.0 copy-done.4
  68.0 0.0 copy-done.10
  68.0 0.9 copy-done.14
  68.9 0.2 multiply_reduce_fusion.2
  69.1 0.0 copy-start.39
  69.1 0.6 copy-done.39
  69.6 2.5 %fusion.38 = (f32[]{:T(128)}, f32[256]{0:T(256)}, f32[256]{0:T(256)}) fusion(s32[]{:T(128)} %bitcast.7, s32[]{:T(128)} %bitcast.6, s32[]{:T(128)S(6)} %mul.251, f32[256]{0:T(256)S(1)} %multiply_reduce_fusion.2), kind=kLoop, calls=%fused_computation.79 | loop fusion | flops 2047 | bytes 3088 | tf_op jit(solution)/shard_map/reduce_sum | solution.py:860
  72.8 7.0 %fusion.8 = (bf16[256,3072]{1,0:T(8,128)(2,1)S(1)}, f32[256,3072]{1,0:T(8,128)S(1)}) fusion(f32[256,3072]{1,0:T(8,128)} %fusion.43, bf16[768,3072]{1,0:T(8,128)(2,1)} %param.20, f32[256,768]{1,0:T(8,128)} %copy-done.14, f32[768]{0:T(1024)S(1)} %copy-done.29, f32[768]{0:T(1024)S(1)} %copy-done.28, f32[256]{0:T(256)} %get-tuple-element.68, ...), kind=kOutput, calls=%fused_computation.14 | convolution fusion | flops 1224671232 | bytes 13377536 | tf_op jit(solution)/shard_map/dot_general | solution.py:850
  79.8 0.0 copy-start.35
  79.8 0.0 copy-start.43
  79.8 5.5 %fusion.44 = f32[256,768]{1,0:T(8,128)S(1)} fusion(bf16[256,3072]{1,0:T(8,128)(2,1)S(1)} %get-tuple-element.65, bf16[768,3072]{1,0:T(8,128)(2,1)} %param.20), kind=kOutput, calls=%fused_computation.85 | convolution fusion | flops 1207959552 | bytes 7077888 | tf_op jit(solution)/shard_map/dot_general | solution.py:44
  85.4 0.0 copy-start.40
  85.4 0.0 copy-start.21
  85.4 5.9 %fusion.21 = (f32[]{:T(128)}, f32[]{:T(128)}, f32[256]{0:T(256)S(1)}, f32[768]{0:T(1024)S(1)}, f32[768]{0:T(1024)S(1)}, /*index=5*/f32[]{:T(128)}, bf16[256,768]{1,0:T(8,128)(2,1)}) fusion(f32[256]{0:T(256)S(1)} %copy-done.43, f32[256,768]{1,0:T(8,128)S(1)} %copy-done.15, f32[256,768]{1,0:T(8,128)S(1)} %fusion.44, f32[768]{0:T(1024)S(1)} %copy-done.28, ...), kind=kOutput, calls=%fused_computation.38 | convolution fusion | flops 1218771200 | bytes 10630156 | tf_op jit(solution)/shard_map/dot_general | solution.py:853
  91.3 0.3 fusion.39
  91.7 0.0 copy-start.17
  91.7 0.6 reshape.132
  92.3 0.6 reshape.133
  92.9 2.0 select_maximum_fusion
  94.9 0.0 copy-done.17
  95.0 0.2 fusion.24
  95.1 0.0 copy-start.23
  95.1 0.7 copy-done.23
  95.9 1.3 fusion.9
  97.1 1.9 copy.23
  99.0 2.7 %convolution_convert_fusion.3.refs_9_ = bf16[768,768]{1,0:T(8,128)(2,1)} fusion(bf16[768,256]{1,0:T(8,128)(2,1)} %bitcast.46, bf16[256,768]{1,0:T(8,128)(2,1)} %copy-done.23), kind=kOutput, calls=%fused_computation.16 | convolution fusion | flops 302579712 | bytes 1966080 | tf_op jit(solution)/shard_map/dot_general | solution.py:870
  101.7 6.5 %convolution_convert_fusion.2.refs_7_ = bf16[3072,768]{1,0:T(8,128)(2,1)} fusion(bf16[256,768]{1,0:T(8,128)(2,1)} %param.12, f32[256,3072]{1,0:T(8,128)} %copy-done.44), kind=kOutput, calls=%fused_computation.2 | convolution fusion | flops 1217396736 | bytes 8257536 | tf_op jit(solution)/shard_map/dot_general | solution.py:38
  108.2 4.0 %convolution_convert_fusion.1.refs_8_ = bf16[768,3072]{1,0:T(8,128)(2,1)} fusion(bf16[256,3072]{1,0:T(8,128)(2,1)S(1)} %copy-done.25, f32[256,768]{1,0:T(8,128)S(1)} %copy-done.16, f32[768]{0:T(1024)S(1)} %copy-done.29, f32[768]{0:T(1024)S(1)} %copy-done.28, f32[256]{0:T(256)S(1)} %copy-done.36, f32[256]{0:T(256)S(1)} %copy-done.34), kind=kOutput, calls=%fused_computation.1 | convolution fusion | flops 1211301888 | bytes 7086080 | tf_op jit(solution)/shard_map/dot_general | solution.py:38
  112.2 72.5 %shard_map.195 = (bf16[3,12,64,256]{3,2,1,0:T(8,128)(2,1)}, bf16[768,384]{1,0:T(8,128)(2,1)}, bf16[192,1536]{1,0:T(8,128)(2,1)}, bf16[192,384]{1,0:T(8,128)(2,1)}) custom-call(bf16[12,64,256]{2,1,0:T(8,128)(2,1)} %bitcast.47, bf16[3,12,64,256]{3,2,1,0:T(8,128)(2,1)} %bitcast.43, bf16[3,4,64,256]{3,2,1,0:T(8,128)(2,1)} %copy-done.7, ...), custom_call_target="tpu_custom_call" | custom-call | tf_op jit(solution)/shard_map/pallas_call | solution.py:690
  184.8 0.0 copy-start.22
  184.8 2.6 %fusion.37 = (f32[768]{0:T(1024)S(1)}, f32[256]{0:T(256)S(1)}, f32[256,768]{1,0:T(8,128)S(1)}) fusion(f32[768]{0:T(1024)S(1)} %copy-done.27, f32[256]{0:T(256)S(1)} %broadcast_multiply_fusion.1, bf16[256,768]{1,0:T(8,128)(2,1)S(1)} %copy-done.13, bf16[2304,256]{1,0:T(8,128)(2,1)} %bitcast.48, bf16[768,2304]{1,0:T(8,128)(2,1)S(1)} %copy-done), kind=kOutput, calls=%fused_computation.78 | convolution fusion | flops 907148288 | bytes 5906432 | tf_op jit(solution)/shard_map/dot_general | solution.py:883
  187.4 0.0 copy-start.30
  187.4 0.6 reshape.131
  188.0 0.4 fusion.18
  188.5 0.6 reshape.130
  189.1 1.1 add_convert_fusion
  190.2 1.4 stack.34.refs_1_
  191.6 0.0 copy-start.9
  191.6 2.8 %convolution_convert_fusion.refs_0_ = bf16[768,2304]{1,0:T(8,128)(2,1)S(1)} fusion(bf16[2304,256]{1,0:T(8,128)(2,1)} %bitcast.49, bf16[256,768]{1,0:T(8,128)(2,1)} %param.11, f32[768]{0:T(1024)S(1)} %copy-done.30, f32[768]{0:T(1024)S(1)} %copy-done.27, f32[256]{0:T(256)} %copy-done.31, f32[256]{0:T(256)S(1)} %broadcast_multiply_fusion.1), kind=kOutput, calls=%fused_computation | convolution fusion | flops 908918784 | bytes 5120000 | tf_op jit(solution)/shard_map/dot_general | solution.py:880
  194.5 43.4 %shard_map.196 = (f32[24,2304]{1,0:T(8,128)S(1)}, f32[96,768]{1,0:T(8,128)S(1)}, f32[24,3072]{1,0:T(8,128)S(1)}, f32[24,768]{1,0:T(8,128)S(1)}, f32[8,768]{1,0:T(8,128)S(1)}) custom-call(bf16[768,2304]{1,0:T(8,128)(2,1)S(1)} %convolution_convert_fusion.refs_0_, f32[8,768]{1,0:T(8,128)S(1)} %copy-done.9, bf16[768,384]{1,0:T(8,128)(2,1)S(1)} %copy-done.5, ...), custom_call_target="tpu_custom_call" | custom-call | tf_op jit(solution)/shard_map/pallas_call | solution.py:796
  237.9 0.6 slice.31
  238.5 1.2 sqrt_bitcast_fusion
  239.7 0.6 fusion.31
  240.3 0.6 fusion.30
  240.8 0.6 fusion.29
  241.4 0.6 fusion.28
  242.0 0.7 copy.28
  242.7 0.6 copy.29
  243.3 0.7 copy.30
  244.0 0.7 copy.31
  (78 shorter events, 0.2 us)
Async XLA Ops:
  0.6 3.9 %copy-start = (bf16[768,2304]{1,0:T(8,128)(2,1)S(1)}, bf16[768,2304]{1,0:T(8,128)(2,1)}, u32[]{:S(2)}) copy-start(bf16[768,2304]{1,0:T(8,128)(2,1)} %param.16) | copy-start | bytes 10616836
  3.2 1.3 copy-start.41
  3.2 1.3 copy-start.31
  10.2 5.7 %copy-start.1 = (bf16[2304,256]{1,0:T(8,128)(2,1)S(1)}, bf16[2304,256]{1,0:T(8,128)(2,1)}, u32[]{:S(2)}) copy-start(bf16[2304,256]{1,0:T(8,128)(2,1)} %copy.22) | copy-start | bytes 3538948
  10.2 5.7 %copy-start.11 = (s32[1,2]{1,0:T(1,128)S(1)}, s32[1,2]{1,0:T(1,128)}, u32[]{:S(2)}) copy-start(s32[1,2]{1,0:T(1,128)} %refs_6_.1) | copy-start | bytes 28
  10.2 56.4 %copy-start.12 = (bf16[256,768]{1,0:T(8,128)(2,1)S(1)}, bf16[256,768]{1,0:T(8,128)(2,1)}, u32[]{:S(2)}) copy-start(bf16[256,768]{1,0:T(8,128)(2,1)} %param.11) | copy-start | bytes 1179652
  10.2 56.4 %copy-start.19 = (bf16[768,768]{1,0:T(8,128)(2,1)S(1)}, bf16[768,768]{1,0:T(8,128)(2,1)}, u32[]{:S(2)}) copy-start(bf16[768,768]{1,0:T(8,128)(2,1)} %param.17) | copy-start | bytes 3538948
  15.8 56.9 %copy-start.28 = (f32[768]{0:T(1024)S(1)}, f32[768]{0:T(1024)}, u32[]{:S(2)}) copy-start(f32[768]{0:T(1024)} %param.18) | copy-start | bytes 9220
  15.8 56.9 %copy-start.29 = (f32[768]{0:T(1024)S(1)}, f32[768]{0:T(1024)}, u32[]{:S(2)}) copy-start(f32[768]{0:T(1024)} %param.19) | copy-start | bytes 9220
  64.6 1.2 copy-start.2
  65.8 0.7 copy-start.3
  65.8 2.2 copy-start.4
  65.8 2.2 copy-start.7
  65.8 2.2 copy-start.10
  68.0 0.9 copy-start.14
  68.9 22.5 %copy-start.33 = (f32[256]{0:T(256)}, f32[256]{0:T(256)S(1)}, u32[]{:S(2)}) copy-start(f32[256]{0:T(256)S(1)} %broadcast_multiply_fusion) | copy-start | bytes 3076
  69.1 0.6 copy-start.39
  79.8 5.6 %copy-start.24 = (bf16[256,3072]{1,0:T(8,128)(2,1)}, bf16[256,3072]{1,0:T(8,128)(2,1)S(1)}, u32[]{:S(2)}) copy-start(bf16[256,3072]{1,0:T(8,128)(2,1)S(1)} %get-tuple-element.65) | copy-start | bytes 4718596
  79.8 5.6 %copy-start.44 = (f32[256,3072]{1,0:T(8,128)}, f32[256,3072]{1,0:T(8,128)S(1)}, u32[]{:S(2)}) copy-start(f32[256,3072]{1,0:T(8,128)S(1)} %get-tuple-element.66) | copy-start | bytes 9437188
  79.8 5.6 %copy-start.15 = (f32[256,768]{1,0:T(8,128)S(1)}, f32[256,768]{1,0:T(8,128)}, u32[]{:S(2)}) copy-start(f32[256,768]{1,0:T(8,128)} %copy-done.14) | copy-start | bytes 2359300
  79.8 5.6 %copy-start.26 = (f32[256,768]{1,0:T(8,128)S(1)}, f32[256,768]{1,0:T(8,128)}, u32[]{:S(2)}) copy-start(f32[256,768]{1,0:T(8,128)} %get-tuple-element.64) | copy-start | bytes 2359300
  79.8 5.6 %copy-start.35 = (f32[256]{0:T(256)S(1)}, f32[256]{0:T(256)}, u32[]{:S(2)}) copy-start(f32[256]{0:T(256)} %get-tuple-element.68) | copy-start | bytes 3076
  79.8 5.5 %copy-start.43 = (f32[256]{0:T(256)S(1)}, f32[256]{0:T(256)}, u32[]{:S(2)}) copy-start(f32[256]{0:T(256)} %get-tuple-element.52) | copy-start | bytes 3076
  85.4 6.0 %copy-start.40 = (f32[256]{0:T(256)S(1)}, f32[256]{0:T(256)}, u32[]{:S(2)}) copy-start(f32[256]{0:T(256)} %copy-done.39) | copy-start | bytes 3076
  85.4 9.6 %copy-start.21 = (bf16[256,768]{1,0:T(8,128)(2,1)S(1)}, bf16[256,768]{1,0:T(8,128)(2,1)}, u32[]{:S(2)}) copy-start(bf16[256,768]{1,0:T(8,128)(2,1)} %param.12) | copy-start | bytes 1179652
  91.3 4.6 %copy-start.20 = (bf16[768,768]{1,0:T(8,128)(2,1)S(1)}, bf16[768,768]{1,0:T(8,128)(2,1)}, u32[]{:S(2)}) copy-start(bf16[768,768]{1,0:T(8,128)(2,1)} %param.17) | copy-start | bytes 3538948
  91.7 3.3 %copy-start.17 = (f32[256,768]{1,0:T(8,128)}, f32[256,768]{1,0:T(8,128)S(1)}, u32[]{:S(2)}) copy-start(f32[256,768]{1,0:T(8,128)S(1)} %get-tuple-element.54) | copy-start | bytes 2359300
  91.7 3.3 %copy-start.37 = (f32[256]{0:T(256)}, f32[256]{0:T(256)S(1)}, u32[]{:S(2)}) copy-start(f32[256]{0:T(256)S(1)} %negate_multiply_fusion.1) | copy-start | bytes 3076
  95.1 0.7 copy-start.23
  101.7 6.5 %copy-start.16 = (f32[256,768]{1,0:T(8,128)S(1)}, f32[256,768]{1,0:T(8,128)}, u32[]{:S(2)}) copy-start(f32[256,768]{1,0:T(8,128)} %copy-done.14) | copy-start | bytes 2359300
  101.7 6.5 %copy-start.25 = (bf16[256,3072]{1,0:T(8,128)(2,1)S(1)}, bf16[256,3072]{1,0:T(8,128)(2,1)}, u32[]{:S(2)}) copy-start(bf16[256,3072]{1,0:T(8,128)(2,1)} %copy-done.24) | copy-start | bytes 4718596
  101.7 6.5 %copy-start.34 = (f32[256]{0:T(256)S(1)}, f32[256]{0:T(256)}, u32[]{:S(2)}) copy-start(f32[256]{0:T(256)} %copy-done.33) | copy-start | bytes 3076
  101.7 6.5 %copy-start.36 = (f32[256]{0:T(256)S(1)}, f32[256]{0:T(256)}, u32[]{:S(2)}) copy-start(f32[256]{0:T(256)} %get-tuple-element.68) | copy-start | bytes 3076
  112.2 72.5 %copy-start.13 = (bf16[256,768]{1,0:T(8,128)(2,1)S(1)}, bf16[256,768]{1,0:T(8,128)(2,1)}, u32[]{:S(2)}) copy-start(bf16[256,768]{1,0:T(8,128)(2,1)} %param.11) | copy-start | bytes 1179652
  112.2 72.5 %copy-start.27 = (f32[768]{0:T(1024)S(1)}, f32[768]{0:T(1024)}, u32[]{:S(2)}) copy-start(f32[768]{0:T(1024)} %param.14) | copy-start | bytes 9220
  184.8 3.2 %copy-start.42 = (f32[256]{0:T(256)S(1)}, f32[256]{0:T(256)}, u32[]{:S(2)}) copy-start(f32[256]{0:T(256)} %copy-done.41) | copy-start | bytes 3076
  184.8 3.3 %copy-start.32 = (f32[256]{0:T(256)S(1)}, f32[256]{0:T(256)}, u32[]{:S(2)}) copy-start(f32[256]{0:T(256)} %copy-done.31) | copy-start | bytes 3076
  184.8 4.3 %copy-start.18 = (f32[256,768]{1,0:T(8,128)S(1)}, f32[256,768]{1,0:T(8,128)}, u32[]{:S(2)}) copy-start(f32[256,768]{1,0:T(8,128)} %copy-done.17) | copy-start | bytes 2359300
  184.8 4.3 %copy-start.22 = (bf16[256,768]{1,0:T(8,128)(2,1)S(1)}, bf16[256,768]{1,0:T(8,128)(2,1)}, u32[]{:S(2)}) copy-start(bf16[256,768]{1,0:T(8,128)(2,1)} %param.12) | copy-start | bytes 1179652
  184.8 4.3 %copy-start.38 = (f32[256]{0:T(256)S(1)}, f32[256]{0:T(256)}, u32[]{:S(2)}) copy-start(f32[256]{0:T(256)} %copy-done.37) | copy-start | bytes 3076
  187.4 4.2 %copy-start.30 = (f32[768]{0:T(1024)S(1)}, f32[768]{0:T(1024)}, u32[]{:S(2)}) copy-start(f32[768]{0:T(1024)} %param.15) | copy-start | bytes 9220
  191.6 2.8 %copy-start.5 = (bf16[768,384]{1,0:T(8,128)(2,1)S(1)}, bf16[768,384]{1,0:T(8,128)(2,1)}, u32[]{:S(2)}) copy-start(bf16[768,384]{1,0:T(8,128)(2,1)} %get-tuple-element.31.refs_2_) | copy-start | bytes 1769476
  191.6 2.8 %copy-start.6 = (bf16[192,1536]{1,0:T(8,128)(2,1)S(1)}, bf16[192,1536]{1,0:T(8,128)(2,1)}, u32[]{:S(2)}) copy-start(bf16[192,1536]{1,0:T(8,128)(2,1)} %get-tuple-element.32.refs_3_) | copy-start | bytes 1769476
  191.6 2.9 %copy-start.8 = (bf16[192,384]{1,0:T(8,128)(2,1)S(1)}, bf16[192,384]{1,0:T(8,128)(2,1)}, u32[]{:S(2)}) copy-start(bf16[192,384]{1,0:T(8,128)(2,1)} %get-tuple-element.33.refs_4_) | copy-start | bytes 442372
  191.6 2.9 %copy-start.9 = (f32[8,768]{1,0:T(8,128)S(1)}, f32[8,768]{1,0:T(8,128)}, u32[]{:S(2)}) copy-start(f32[8,768]{1,0:T(8,128)} %stack.34.refs_1_) | copy-start | bytes 73732

commit v3 on v0

--- a/solution.py
+++ b/solution.py
@@ -1,11 +1,16 @@
+import functools
+
 import jax
 import jax.numpy as jnp
 from jax import lax
+from jax.experimental import pallas as pl
+from jax.experimental.pallas import tpu as pltpu
 from jax.sharding import PartitionSpec as P
 
 D = 768
 HEADS = 12
 HEAD_DIM = 64
+MESH = pl.DeviceIdType.MESH
 
 
 epsilon = 1e-05
@@ -272,6 +277,891 @@
     )
 
 
+def rows_of(start, count):
+    return pl.ds(pl.multiple_of(start, 16), count)
+
+
+def matmul(left, right):
+    return jnp.dot(left, right, preferred_element_type=jnp.float32)
+
+
+def signed_terms(scores):
+    square = scores * scores + 1.0
+    inverse = lax.rsqrt(square)
+    return inverse, scores * inverse, jnp.exp(square * inverse)
+
+
+def valid_columns(span, start, count):
+    pos = start + lax.broadcasted_iota(jnp.int32, (1, count), 1)
+    return (pos >= span[0, 0]) & (pos < span[0, 1])
+
+
+def greet(partners):
+    barrier = pltpu.get_barrier_semaphore()
+    for partner in partners:
+        pl.semaphore_signal(barrier, inc=1, device_id=partner, device_id_type=MESH)
+    pl.semaphore_wait(barrier, len(partners))
+
+
+def sender(send_sems, recv_sems):
+    count = [0]
+
+    def send(src, dst, target):
+        slot = count[0]
+        count[0] += 1
+        copy = pltpu.make_async_remote_copy(
+            src_ref=src, dst_ref=dst, send_sem=send_sems.at[slot], recv_sem=recv_sems.at[slot],
+            device_id=target, device_id_type=MESH,
+        )
+        copy.start()
+        return copy
+
+    return send
+
+
+def place():
+    grp, seq = lax.axis_index("grp"), lax.axis_index("seq")
+    zed, core = seq // 2, seq % 2
+    sibling = (grp, zed * 2 + 1 - core)
+    along = [(zed + k) % 4 for k in range(4)]
+    return grp, seq, zed, core, sibling, along
+
+
+def alone_terms(raw):
+    q, k, v = (raw[part].astype(jnp.float32) for part in range(3))
+    inverse, signed, terms = signed_terms(jnp.sum(q * k, axis=0, keepdims=True))
+    weight = (signed * terms).astype(jnp.bfloat16).astype(jnp.float32)
+    return q, k, v, inverse, signed, terms, weight
+
+
+def attend_kernel(
+    x, gain, bias, w_qkv, span, mixed_out, q_all, kv_all, raw, mix_all, tot_all, norm_all,
+    windows, weights, keys, mixes, totals, leaving, load, hop_send, hop_recv, swap_send, swap_recv, back_send, back_recv,
+):
+    tokens, width = x.shape
+    f32, bf16 = jnp.float32, jnp.bfloat16
+    grp, seq, zed, core, sibling, along = place()
+
+    start = pl.multiple_of(zed * 192 // 128 * 128, 128)
+    inside = pl.ds(pl.multiple_of(zed % 2 * HEAD_DIM, HEAD_DIM), 3 * HEAD_DIM)
+    loads = []
+    for part in range(3):
+        window = w_qkv.at[:, pl.ds(pl.multiple_of(part * width + start, 128), 256)]
+        loads.append(pltpu.make_async_copy(window, windows.at[part], load.at[part]))
+        loads[-1].start()
+    greet_line(grp, zed, core)
+    vector = x[...].astype(f32)
+    centered = vector - jnp.mean(vector, axis=-1, keepdims=True)
+    variance = jnp.mean(centered * centered, axis=-1, keepdims=True)
+    normed = (
+        centered * lax.rsqrt(variance + epsilon) * gain[...].reshape(1, width)
+        + bias[...].reshape(1, width)
+    ).astype(bf16)
+    norm_all[zed] = normed.T
+
+    def hop(step, side):
+        towards = 1 - 2 * side
+        block = zed - towards * step
+        runs = (block >= 0) & (block < 4) & (zed + towards >= 0) & (zed + towards < 4)
+        copy = pltpu.make_async_remote_copy(
+            src_ref=norm_all.at[block], dst_ref=norm_all.at[block],
+            send_sem=hop_send.at[side, step], recv_sem=hop_recv.at[side, step],
+            device_id=(grp, (zed + towards) * 2 + core), device_id_type=MESH,
+        )
+        return runs, copy
+
+    def hop_on(step):
+        for side in range(2):
+            runs, copy = hop(step, side)
+            pl.when(runs)(copy.start)
+
+    hop_on(0)
+    for part in range(3):
+        loads[part].wait()
+        weights[part] = windows[part].T
+    no_score = signed_terms(jnp.zeros((1, tokens), f32))[2]
+    extra = span[0, 0].astype(f32) * no_score
+    mixes[...] = jnp.zeros(mixes.shape, f32)
+    totals[...] = jnp.zeros(totals.shape, f32)
+
+    def swap(block, slot):
+        return pltpu.make_async_remote_copy(
+            src_ref=kv_all.at[:, block, core], dst_ref=kv_all.at[:, block, core],
+            send_sem=swap_send.at[slot], recv_sem=swap_recv.at[slot],
+            device_id=sibling, device_id_type=MESH,
+        )
+
+    def project(block, slot):
+        keep = valid_columns(span, (2 * block + core) * tokens, tokens).astype(f32)
+        for part in range(3):
+            heads = matmul(weights[part, inside, :], norm_all[block])
+            if part == 0:
+                heads = heads * 0.125
+            for h in range(3):
+                one = heads[h * HEAD_DIM : (h + 1) * HEAD_DIM]
+                raw[block, 3 * h + part] = one.astype(bf16)
+                if part == 0:
+                    q_all[h, block] = (one * keep).astype(bf16)
+                else:
+                    kv_all[h, block, core, part - 1] = (one * keep).astype(bf16)
+        swap(block, slot).start()
+
+    def turn(block, slot):
+        swap(block, slot).wait_recv()
+        for h in range(3):
+            for side in range(2):
+                keys[h, block, side * tokens : (side + 1) * tokens, :] = kv_all[h, block, side, 0].T
+
+    def pair(block, other, last):
+        results = []
+        for h in range(3):
+            queries = q_all[h, block]
+            total, mixed = totals[h, block], mixes[h, block]
+            for side in range(2):
+                scores = matmul(keys[h, other, side * tokens : (side + 1) * tokens, :], queries)
+                _, signed, terms = signed_terms(scores)
+                if last:
+                    key_pos = lax.broadcasted_iota(jnp.int32, scores.shape, 0)
+                    query_pos = lax.broadcasted_iota(jnp.int32, scores.shape, 1)
+                    seen = key_pos + side * tokens <= query_pos + core * tokens
+                    terms = jnp.where(seen, terms, 0.0)
+                total = total + jnp.sum(terms.reshape(tokens // 8, 8, tokens), axis=0)
+                mixed = mixed + matmul(kv_all[h, other, side, 1], (signed * terms).astype(bf16))
+            results.append((total, mixed))
+        for h, (total, mixed) in enumerate(results):
+            totals[h, block], mixes[h, block] = total, mixed
+
+    def back(block):
+        return pltpu.make_async_remote_copy(
+            src_ref=leaving.at[block], dst_ref=mixed_out.at[pl.ds(3 * zed, 3)],
+            send_sem=back_send.at[block], recv_sem=back_recv.at[zed],
+            device_id=(grp, block * 2 + core), device_id_type=MESH,
+        )
+
+    def complete(block):
+        fine = valid_columns(span, (2 * block + core) * tokens, tokens)
+        for h in range(3):
+            total = jnp.sum(totals[h, block], axis=0, keepdims=True) - extra
+            total = jnp.where(fine, total, 1.0)
+            mixed = mixes[h, block] / total
+            mix_all[h, block] = mixed
+            tot_all[h, block] = total
+            _, _, v, _, _, terms, weight = alone_terms(raw.at[block, pl.ds(3 * h, 3)])
+            leaving[block, h] = jnp.where(fine, mixed, weight * v / terms).astype(bf16)
+
+        @pl.when(block != zed)
+        def _():
+            back(block).start()
+
+        @pl.when(block == zed)
+        def _():
+            mixed_out[pl.ds(3 * zed, 3)] = leaving[zed]
+
+    project(zed, 0)
+    turn(zed, 0)
+    pair(zed, zed, True)
+
+    @pl.when(zed == 0)
+    def _():
+        complete(0)
+
+    def step(d, _):
+        low, high = zed - d, zed + d
+        for side, block in ((0, low), (1, high)):
+
+            @pl.when((block >= 0) & (block < 4))
+            def _():
+                towards = 1 - 2 * side
+                pltpu.make_async_remote_copy(
+                    src_ref=norm_all.at[block], dst_ref=norm_all.at[block],
+                    send_sem=hop_send.at[side, d - 1], recv_sem=hop_recv.at[side, d - 1],
+                    device_id=(grp, (zed - towards) * 2 + core), device_id_type=MESH,
+                ).wait_recv()
+                runs, copy = hop(d, side)
+                pl.when(runs)(copy.start)
+                project(block, 2 * d + side)
+
+        @pl.when(high < 4)
+        def _():
+            lax.fori_loop(jnp.maximum(low + 1, 0), high, lambda j, _: (pair(high, j, False), 0)[1], 0)
+            turn(high, 2 * d + 1)
+            pair(high, high, True)
+
+        @pl.when(low >= 0)
+        def _():
+            turn(low, 2 * d)
+            pair(low, low, True)
+
+            @pl.when(high < 4)
+            def _():
+                pair(high, low, False)
+
+            pl.when(low == 0)(lambda: complete(low))
+
+            def later(i, _):
+                pair(i, low, False)
+                pl.when(low == 0)(lambda: complete(i))
+                return 0
+
+            lax.fori_loop(low + 1, jnp.minimum(high, 4), later, 0)
+
+        @pl.when((high < 4) & (low <= 0))
+        def _():
+            complete(high)
+
+        return 0
+
+    lax.fori_loop(1, 4, step, 0)
+
+    for k in (1, 2, 3):
+        back(along[k]).wait_send()
+        pltpu.make_async_remote_copy(
+            src_ref=leaving.at[zed], dst_ref=mixed_out.at[pl.ds(3 * along[k], 3)],
+            send_sem=back_send.at[zed], recv_sem=back_recv.at[along[k]],
+            device_id=(grp, along[k] * 2 + core), device_id_type=MESH,
+        ).wait_recv()
+    for d in range(4):
+        for side in range(2):
+            runs, copy = hop(d, side)
+            pl.when(runs)(copy.wait_send)
+            if d > 0 or side == 0:
+                block = zed + (2 * side - 1) * d
+                pl.when((block >= 0) & (block < 4))(swap(block, 2 * d + side).wait_send)
+
+
+def greet_line(grp, zed, core):
+    partners = [(grp, zed * 2 + 1 - core)]
+    partners += [(grp, (zed + k) % 4 * 2 + core) for k in (1, 2, 3)]
+    greet(partners)
+
+
+def attend(block_input, gain, bias, w_qkv, span):
+    f32, bf16 = jnp.float32, jnp.bfloat16
+    tokens, width = block_input.shape
+    vmem, smem = pl.BlockSpec(memory_space=pltpu.VMEM), pl.BlockSpec(memory_space=pltpu.SMEM)
+    block = (HEAD_DIM, tokens)
+    dma = pltpu.SemaphoreType.DMA
+    return pl.pallas_call(
+        attend_kernel,
+        out_shape=[
+            jax.ShapeDtypeStruct((HEADS,) + block, bf16),
+            jax.ShapeDtypeStruct((3, 4) + block, bf16),
+            jax.ShapeDtypeStruct((3, 4, 2, 2) + block, bf16),
+            jax.ShapeDtypeStruct((4, 9) + block, bf16),
+            jax.ShapeDtypeStruct((3, 4) + block, f32),
+            jax.ShapeDtypeStruct((3, 4, 1, tokens), f32),
+            jax.ShapeDtypeStruct((4, width, tokens), bf16),
+        ],
+        in_specs=[vmem] * 3 + [pl.BlockSpec(memory_space=pl.ANY), smem],
+        out_specs=[vmem] * 7,
+        scratch_shapes=[
+            pltpu.VMEM((3, width, 256), bf16),
+            pltpu.VMEM((3, 256, width), bf16),
+            pltpu.VMEM((3, 4, 2 * tokens, HEAD_DIM), bf16),
+            pltpu.VMEM((3, 4) + block, f32),
+            pltpu.VMEM((3, 4, 8, tokens), f32),
+            pltpu.VMEM((4, 3) + block, bf16),
+            dma((3,)),
+            dma((2, 4)),
+            dma((2, 4)),
+            dma((8,)),
+            dma((8,)),
+            dma((4,)),
+            dma((4,)),
+        ],
+        compiler_params=pltpu.CompilerParams(
+            collective_id=1, has_side_effects=True, vmem_limit_bytes=48 * 2**20
+        ),
+    )(block_input, gain, bias, w_qkv, span)
+
+
+def gelu_and_slope(u):
+    root = 0.7978845608028654
+    square = u * u
+    bent = jnp.tanh(root * (u + 0.044715 * (square * u)))
+    half = 0.5 * (1.0 + bent)
+    slope = half + 0.5 * u * (1.0 - bent * bent) * (root * (1.0 + 0.134145 * square))
+    return u * half, slope
+
+
+def normal_parts(vector):
+    centered = vector - jnp.mean(vector, axis=-1, keepdims=True)
+    variance = jnp.mean(centered * centered, axis=-1, keepdims=True)
+    inverse = lax.rsqrt(variance + epsilon)
+    return centered * inverse, inverse
+
+
+def norm_pull(normal, inverse, gain, grad):
+    scaled = grad * gain
+    along_normal = jnp.mean(scaled * normal, axis=-1, keepdims=True)
+    return inverse * (scaled - jnp.mean(scaled, axis=-1, keepdims=True) - normal * along_normal)
+
+
+def middle_kernel(
+    chunk, mixed, x, out_grad, w_out, w_up, w_down, gain, bias, span,
+    block_output, grad_middle, grad_mixed, term_down, term_up, term_out, small,
+    middle, normed, normed_t, mlp_out, grad_norm,
+):
+    tokens, width = x.shape
+    f32, bf16 = jnp.float32, jnp.bfloat16
+    seq = lax.axis_index("seq")
+    pos = seq * tokens + lax.broadcasted_iota(jnp.int32, (tokens, 1), 0)
+    keep = ((pos >= span[0, 0]) & (pos < span[0, 1])).astype(f32)
+    gain_row, bias_row = gain[...].reshape(1, width), bias[...].reshape(1, width)
+
+    def squares(value):
+        return jnp.sum(keep * value * value)
+
+    attn_out = matmul(mixed[...].T, w_out[...])
+    attn_squares = squares(attn_out)
+    middle[...] = x[...].astype(f32) + attn_out
+    normed[...] = (normal_parts(middle[...])[0] * gain_row + bias_row).astype(bf16)
+    normed_t[...] = normed[...].T
+    mlp_out[...] = jnp.zeros((tokens, width), f32)
+    grad_norm[...] = jnp.zeros((tokens, width), f32)
+
+    def hidden(i, _):
+        at = pl.ds(pl.multiple_of(i * chunk, chunk), chunk)
+        activated, slope = gelu_and_slope(matmul(normed[...], w_up[:, at]))
+        activated = activated.astype(bf16)
+        mlp_out[...] += matmul(activated, w_down[at, :])
+        grad_up = (contract_cols(out_grad[...], w_down[at, :]) * slope).astype(bf16)
+        grad_norm[...] += contract_cols(grad_up, w_up[:, at])
+        term_up[:, at] = matmul(normed_t[...], grad_up).astype(bf16)
+        term_down[at, :] = matmul(activated.T, out_grad[...]).astype(bf16)
+        return 0
+
+    lax.fori_loop(0, w_up.shape[1] // chunk, hidden, 0)
+    output = middle[...] + mlp_out[...]
+    block_output[...] = output.astype(bf16)
+    sums = [squares(output), attn_squares, squares(mlp_out[...]), jnp.sum(keep) * width]
+    normal, inverse = normal_parts(middle[...])
+    grad = grad_norm[...]
+    grad_middle[...] = out_grad[...].astype(f32) + norm_pull(normal, inverse, gain_row, grad)
+    small[0:2] = jnp.zeros((2, width), f32)
+    small[2:3] = jnp.sum(grad * normal, axis=0, keepdims=True)
+    small[3:4] = jnp.sum(grad, axis=0, keepdims=True)
+    lane = lax.broadcasted_iota(jnp.int32, (4, width), 1)
+    row = jnp.zeros((4, width), f32)
+    for i, value in enumerate(sums):
+        row = jnp.where(lane == i, value, row)
+    small[4:8] = row
+    grad_attn = grad_middle[...].astype(bf16)
+    grad_mixed[...] = contract_cols(w_out[...], grad_attn).astype(bf16)
+    term_out[...] = matmul(mixed[...], grad_attn).astype(bf16)
+
+
+def middle_part(mixed, block_input, out_grad, w_out, w_up, w_down, gain, bias, span):
+    f32, bf16 = jnp.float32, jnp.bfloat16
+    tokens, width = block_input.shape
+    vmem, smem = pl.BlockSpec(memory_space=pltpu.VMEM), pl.BlockSpec(memory_space=pltpu.SMEM)
+    return pl.pallas_call(
+        functools.partial(middle_kernel, 512),
+        out_shape=[
+            jax.ShapeDtypeStruct((tokens, width), bf16),
+            jax.ShapeDtypeStruct((tokens, width), f32),
+            jax.ShapeDtypeStruct((width, tokens), bf16),
+            jax.ShapeDtypeStruct(w_down.shape, bf16),
+            jax.ShapeDtypeStruct(w_up.shape, bf16),
+            jax.ShapeDtypeStruct(w_out.shape, bf16),
+            jax.ShapeDtypeStruct((8, width), f32),
+        ],
+        in_specs=[vmem] * 8 + [smem],
+        out_specs=[vmem] * 7,
+        scratch_shapes=[
+            pltpu.VMEM((tokens, width), f32),
+            pltpu.VMEM((tokens, width), bf16),
+            pltpu.VMEM((width, tokens), bf16),
+            pltpu.VMEM((tokens, width), f32),
+            pltpu.VMEM((tokens, width), f32),
+        ],
+        compiler_params=pltpu.CompilerParams(vmem_limit_bytes=48 * 2**20),
+    )(mixed, block_input, out_grad, w_out, w_up, w_down, gain, bias, span)
+
+
+def add_rows(into, base, count, *terms):
+    def add(i, _):
+        total = None
+        for ref, start in terms:
+            term = ref[rows_of(start + i * 16, 16), :].astype(jnp.float32)
+            total = term if total is None else total + term
+        into[rows_of(base + i * 16, 16), :] = total.astype(jnp.bfloat16)
+        return 0
+
+    lax.fori_loop(0, count // 16, add, 0)
+
+
+class GroupSum:
+    def __init__(self, term, first, near, held):
+        self.term, self.first, self.near, self.held = term, first, near, held
+        self.rows, self.columns = term.shape[0] // 4, term.shape[1] // 2
+        grp, seq, zed, core, sibling, along = place()
+        self.place_in_plane(grp, seq)
+        self.sibling = sibling
+        self.mine = term.at[:, pl.ds(pl.multiple_of(core * self.columns, 128), self.columns)]
+        self.away = pl.ds(pl.multiple_of((1 - core) * self.columns, 128), self.columns)
+        self.copies = []
+
+    def place_in_plane(self, grp, seq):
+        y, x = grp // 2, grp % 2
+        self.own, self.beside, self.above = grp, y * 2 + 1 - x, (1 - y) * 2 + x
+        self.across = (1 - y) * 2 + 1 - x
+        self.to_x, self.to_y = (self.beside, seq), (self.above, seq)
+
+    def swap(self, send):
+        self.halves = []
+        for quarter in (self.across, self.beside, self.above, self.own):
+            at = rows_of(quarter * self.rows, self.rows)
+            self.halves.append(
+                send(self.term.at[at, self.away], self.first.at[at, :], self.sibling)
+            )
+
+    def part(self, quarter, half):
+        return rows_of(quarter * self.rows + half * (self.rows // 2), self.rows // 2)
+
+    def pass_on(self, send, quarter, half, slot, target):
+        self.copies.append(
+            send(self.first.at[self.part(quarter, half), :], self.near.at[slot], target)
+        )
+
+    def core_sum(self, quarter):
+        base = quarter * self.rows
+        add_rows(self.first, base, self.rows, (self.mine, base), (self.first, base))
+
+    def step_one(self, send):
+        steps = (
+            (self.across, ((0, 0, self.to_x), (1, 2, self.to_y))),
+            (self.beside, ((0, 1, self.to_x),)),
+            (self.above, ((1, 3, self.to_y),)),
+        )
+        for copy, (quarter, passes) in zip(self.halves, steps):
+            copy.wait_recv()
+            self.core_sum(quarter)
+            for half, slot, target in passes:
+                self.pass_on(send, quarter, half, slot, target)
+        self.copies = [self.copies[i] for i in (0, 2, 1, 3)]
+
+    def step_two(self, send):
+        half = self.rows // 2
+        for slot, quarter, side, target in (
+            (0, self.above, 0, self.to_y),
+            (2, self.beside, 1, self.to_x),
+        ):
+            base = quarter * self.rows + side * half
+            self.copies[slot].wait_recv()
+            add_rows(self.first, base, half, (self.first, base), (self.near.at[slot], 0))
+            self.pass_on(send, quarter, side, 4 + side, target)
+
+    def total(self):
+        half = self.rows // 2
+        self.halves[3].wait_recv()
+        for slot in (1, 3, 4, 5):
+            self.copies[slot].wait_recv()
+        for side, one, two in ((0, 1, 4), (1, 3, 5)):
+            base = self.own * self.rows + side * half
+            add_rows(
+                self.held, side * half, half, (self.mine, base), (self.first, base),
+                (self.near.at[one], 0), (self.near.at[two], 0),
+            )
+
+    def drain(self):
+        for copy in self.halves + self.copies:
+            copy.wait_send()
+
+
+class HeadsSum(GroupSum):
+    def __init__(self, term, other, first, near, final):
+        self.term, self.other, self.first, self.near, self.final = term, other, first, near, final
+        self.rows = 4 * term.shape[2]
+        grp, seq, zed, self.core, self.sibling, along = place()
+        self.place_in_plane(grp, seq)
+        self.copies = []
+
+    def swap_quarter(self, send, quarter):
+        at = pl.ds(4 * quarter, 4)
+        return send(self.term.at[at, 1 - self.core], self.other.at[at], self.sibling)
+
+    def both_cores(self, quarter):
+        at = pl.ds(4 * quarter, 4)
+        return (self.term[at, self.core] + self.other[at]).reshape(self.rows, -1)
+
+    def core_sum(self, quarter):
+        self.first[rows_of(quarter * self.rows, self.rows), :] = self.both_cores(quarter).astype(
+            jnp.bfloat16
+        )
+
+    def total(self):
+        self.halves[3].wait_recv()
+        for slot in (1, 3, 4, 5):
+            self.copies[slot].wait_recv()
+        near = [self.near[i].astype(jnp.float32) for i in range(6)]
+        total = self.both_cores(self.own) + jnp.concatenate(
+            [near[1] + near[4], near[3] + near[5]], axis=0
+        )
+        self.final[...] = total.reshape(self.final.shape)
+
+
+def send_line(send, held, third, along, line):
+    rows = held.shape[0] // 4
+    return [
+        send(held.at[rows_of(along[k] * rows, rows), :], third.at[k - 1], line[k - 1])
+        for k in (1, 2, 3)
+    ]
+
+
+def sum_line(send, copies, held, third, mine, out, zed, core, sibling):
+    rows, columns = held.shape[0] // 4, held.shape[1]
+    for copy in copies:
+        copy.wait_recv()
+    total = held[rows_of(zed * rows, rows), :].astype(jnp.float32)
+    for j in range(3):
+        total = total + third[j].astype(jnp.float32)
+    mine[...] = total
+    column = pl.ds(pl.multiple_of(core * columns, 128), columns)
+    half = rows // 2
+    away = pl.ds(pl.multiple_of((1 - core) * half, 8), half)
+    out[:, column] = mine[pl.ds(pl.multiple_of(core * half, 8), half), :]
+    return send(mine.at[away, :], out.at[:, column], sibling)
+
+
+def norm_back(x, gain, grad_norm, grad_out, into, chunk):
+    f32 = jnp.float32
+    tokens, width = x.shape
+    gain_row = gain[...].reshape(1, width)
+
+    def one(i, sums):
+        at = rows_of(i * chunk, chunk)
+        vector, grad = x[at, :].astype(f32), grad_norm[at, :]
+        normal, inverse = normal_parts(vector)
+        pulled = norm_pull(normal, inverse, gain_row, grad)
+        into[at, :] = (grad_out[at, :] + pulled).astype(into.dtype)
+        return (
+            sums[0] + jnp.sum(grad * normal, axis=0, keepdims=True),
+            sums[1] + jnp.sum(grad, axis=0, keepdims=True),
+        )
+
+    zero = jnp.zeros((1, width), f32)
+    return lax.fori_loop(0, tokens // chunk, one, (zero, zero))
+
+
+def settle_small(small, vecs, rms, owner):
+    width, count = small.shape[-1], vecs.shape[-1]
+    total = (small[0] + small[1]) + (small[2] + small[3])
+    turned = pltpu.roll(total, (width - owner * count) % width, 1)
+    for i in range(4):
+        vecs[i] = turned[i : i + 1, :count]
+    rms[...] = jnp.sqrt(total[4:5, :3] / total[4:5, 3:4])
+
+
+def attend_back_kernel(many, *refs):
+    (gmix, q_all, kv_all, raw, mix_all, tot_all, norm_all, span, x, gain, w_qkv, grad_middle,
+     small_in) = refs[:13]
+    terms_in = refs[13 : 13 + many]
+    refs = refs[13 + many :]
+    input_grad, sum_qkv, vecs, rms = refs[:4]
+    outs = refs[4 : 4 + many]
+    rest = refs[4 + many :]
+    first, near, held, third, mine = (rest[i * many : (i + 1) * many] for i in range(5))
+    (gm_in, keys, values, g_all, gt_all, grad_kv, part_out, part_in, leaving, arrived,
+     term, other, first_qkv, near_qkv, final, gathered, grad_norm, small_a, small_b, small_c,
+     send_sems, recv_sems) = rest[5 * many :]
+    tokens, width = x.shape
+    f32, bf16 = jnp.float32, jnp.bfloat16
+    grp, seq, zed, core, sibling, along = place()
+    line = [(grp, along[k] * 2 + core) for k in (1, 2, 3)]
+    sums = [GroupSum(*refs_of) for refs_of in zip(terms_in, first, near, held)]
+    heads_sum = HeadsSum(term, other, first_qkv, near_qkv, final)
+    plane = [heads_sum.to_x, heads_sum.to_y, (heads_sum.across, seq)]
+
+    greet([sibling] + line + plane)
+    send = sender(send_sems, recv_sems)
+    coming = []
+    for h in range(3):
+        for k in (1, 2, 3):
+            coming.append(send(gmix.at[along[k] * 3 + h], gm_in.at[h, zed], line[k - 1]))
+    for each in sums:
+        each.swap(send)
+    for h in range(3):
+        gm_in[h, zed] = gmix[zed * 3 + h]
+
+    def turn(i, _):
+        h, z = i // 4, i % 4
+        for side in range(2):
+            at = pl.ds(side * tokens, tokens)
+            keys[h, z, at, :] = kv_all[h, z, side, 0].T
+            values[h, z, at, :] = kv_all[h, z, side, 1].T
+        return 0
+
+    lax.fori_loop(0, 12, turn, 0)
+    for z in range(4):
+        leaving[z, 9] = jnp.zeros((HEAD_DIM, tokens), bf16)
+    sums[0].step_one(send)
+
+    swaps, sends = [], []
+
+    def finish(h):
+        swaps[h].wait_recv()
+
+        def merge(z, _):
+            fine = valid_columns(span, (2 * z + core) * tokens, tokens)
+            q, k, v, inverse, signed, terms, weight = alone_terms(raw.at[z, pl.ds(3 * h, 3)])
+            g = gm_in[h, z].astype(f32)
+            total = 1.0 / terms
+            grad_total = -jnp.sum(g * (weight * v), axis=0, keepdims=True) * total * total
+            g = (g * total).astype(bf16).astype(f32)
+            grad_weight = jnp.sum(g * v, axis=0, keepdims=True)
+            slope = 1.0 + (inverse * inverse) * (inverse - 1.0)
+            grad_score = terms * (grad_weight * slope + grad_total * signed)
+            grad_score = grad_score.astype(bf16).astype(f32)
+            alone = (grad_score * k * 0.125, grad_score * q, weight * g)
+            parts = [leaving[z, 3 * h].astype(f32)]
+            for part in range(2):
+                parts.append(grad_kv[h, z, core, part] + part_in[h, z, part].astype(f32))
+            for part in range(3):
+                leaving[z, 3 * h + part] = jnp.where(fine, parts[part], alone[part]).astype(bf16)
+            return 0
+
+        lax.fori_loop(0, 4, merge, 0)
+        at = pl.ds(3 * h, 3)
+        for k in (1, 2, 3):
+            sends.append(
+                send(leaving.at[along[k], at], arrived.at[:, zed * 3 + h], line[k - 1])
+            )
+        for part in range(3):
+            arrived[part, zed * 3 + h] = leaving[zed, 3 * h + part]
+
+    for h in range(3):
+        for copy in coming[h * 3 : h * 3 + 3]:
+            copy.wait_recv()
+
+        def prepare(z, _):
+            g = gm_in[h, z].astype(f32)
+            total = 1.0 / tot_all[h, z]
+            g_all[z] = (g * total).astype(bf16)
+            gt_all[z] = -jnp.sum(g * mix_all[h, z], axis=0, keepdims=True) * total
+            for side in range(2):
+                for part in range(2):
+                    grad_kv[h, z, side, part] = jnp.zeros((HEAD_DIM, tokens), f32)
+            return 0
+
+        lax.fori_loop(0, 4, prepare, 0)
+
+        def query_block(z, _):
+            queries, grads, grad_total = q_all[h, z], g_all[z], gt_all[z]
+
+            def pair(other_z, grad_query, last=False):
+                for side in range(2):
+                    at = pl.ds(side * tokens, tokens)
+                    scores = matmul(keys[h, other_z, at, :], queries)
+                    grad_weights = matmul(values[h, other_z, at, :], grads)
+                    inverse, signed, terms = signed_terms(scores)
+                    if last:
+                        key_pos = lax.broadcasted_iota(jnp.int32, scores.shape, 0)
+                        query_pos = lax.broadcasted_iota(jnp.int32, scores.shape, 1)
+                        seen = key_pos + side * tokens <= query_pos + core * tokens
+                        terms = jnp.where(seen, terms, 0.0)
+                    weights = (signed * terms).astype(bf16)
+                    slope = 1.0 + (inverse * inverse) * (inverse - 1.0)
+                    grad_scores = terms * (grad_weights * slope + grad_total * signed)
+                    grad_scores = grad_scores.astype(bf16)
+                    grad_query = grad_query + matmul(kv_all[h, other_z, side, 0], grad_scores)
+                    grad_kv[h, other_z, side, 0] += contract_cols(queries, grad_scores)
+                    grad_kv[h, other_z, side, 1] += contract_cols(grads, weights)
+                return grad_query
+
+            zero = jnp.zeros((HEAD_DIM, tokens), f32)
+            grad_query = pair(z, lax.fori_loop(0, z, pair, zero), True)
+            leaving[z, 3 * h] = (grad_query * 0.125).astype(bf16)
+            return 0
+
+        lax.fori_loop(0, 2, query_block, 0)
+        if h > 0:
+            finish(h - 1)
+        if h == 2:
+            sums[1].step_two(send)
+        lax.fori_loop(2, 4, query_block, 0)
+
+        def pack(z, _):
+            for part in range(2):
+                part_out[h, z, part] = grad_kv[h, z, 1 - core, part].astype(bf16)
+            return 0
+
+        lax.fori_loop(0, 4, pack, 0)
+        swaps.append(send(part_out.at[h], part_in.at[h], sibling))
+        if h == 0:
+            sums[1].step_one(send)
+        if h == 1:
+            sums[0].step_two(send)
+            sums[2].step_one(send)
+    finish(2)
+    sums[0].total()
+    lines = [send_line(send, held[0], third[0], along, line)]
+
+    heads_sum.halves = []
+    for quarter in (heads_sum.across, heads_sum.beside, heads_sum.above, heads_sum.own):
+        total = None
+        for z in range(4):
+            rows = norm_all[z, rows_of(quarter * (width // 4), width // 4), :]
+            part = contract_cols(rows, leaving[z].reshape(10 * HEAD_DIM, tokens))
+            total = part if total is None else total + part
+        term[pl.ds(4 * quarter, 4)] = total.reshape((4,) + term.shape[1:])
+        heads_sum.halves.append(heads_sum.swap_quarter(send, quarter))
+    sums[2].step_two(send)
+    heads_sum.step_one(send)
+    for a in range(1, many):
+        sums[a].total()
+        lines.append(send_line(send, held[a], third[a], along, line))
+
+    for copy in sends:
+        copy.wait_recv()
+    grads = arrived[...].reshape(3 * width, tokens)
+    for i in range(width // 256):
+        columns = slice(i * 256, (i + 1) * 256)
+        grad_norm[:, columns] = matmul(w_qkv[columns, :], grads).T
+    gain_grad, bias_grad = norm_back(x, gain, grad_norm, grad_middle, input_grad, 64)
+    small_a[0] = small_in[...]
+    small_a[0, 0:1] = gain_grad
+    small_a[0, 1:2] = bias_grad
+    swap = send(small_a.at[0], small_a.at[1], sibling)
+    heads_sum.step_two(send)
+    swap.wait()
+    small_b[pl.ds(grp, 1)] = small_a[0:1] + small_a[1:2]
+    across = [(k, seq) for k in (heads_sum.beside, heads_sum.above, heads_sum.across)]
+    planes = [send(small_b.at[grp], small_b.at[grp], target) for target in across]
+    heads_sum.total()
+    gathered[pl.ds(zed, 1)] = final[pl.ds(zed, 1)]
+    blocks = [send(final.at[along[k]], gathered.at[zed], line[k - 1]) for k in (1, 2, 3)]
+    for copy in planes:
+        copy.wait_recv()
+    small_c[pl.ds(zed, 1)] = (small_b[0:1] + small_b[1:2]) + (small_b[2:3] + small_b[3:4])
+    columns = [send(small_c.at[zed], small_c.at[zed], line[k - 1]) for k in (1, 2, 3)]
+    ends = []
+    for a in range(many):
+        ends.append(
+            sum_line(send, lines[a], held[a], third[a], mine[a], outs[a], zed, core, sibling)
+        )
+    for copy in blocks + columns:
+        copy.wait_recv()
+    for z in range(4):
+        for h in range(3):
+            for part in range(3):
+                start = part * width + (3 * z + h) * HEAD_DIM
+                sum_qkv[:, start : start + HEAD_DIM] = gathered[
+                    z, :, (3 * h + part) * HEAD_DIM : (3 * h + part + 1) * HEAD_DIM
+                ]
+    settle_small(small_c, vecs, rms, grp * 8 + seq)
+    for copy in ends:
+        copy.wait_recv()
+    for copy in coming + swaps + sends + planes + blocks + columns + ends:
+        copy.wait_send()
+    for copies in lines:
+        for copy in copies:
+            copy.wait_send()
+    for each in sums + [heads_sum]:
+        each.drain()
+
+
+def attend_back(gmix, saved, span, block_input, gain, w_qkv, grad_middle, small, terms):
+    f32, bf16 = jnp.float32, jnp.bfloat16
+    tokens, width = block_input.shape
+    many = len(terms)
+    vmem, smem = pl.BlockSpec(memory_space=pltpu.VMEM), pl.BlockSpec(memory_space=pltpu.SMEM)
+    block = (HEAD_DIM, tokens)
+    copies = 9 + 10 * many + 3 + 9 + 10 + 1 + 3 * many + 3 + 3 + 3 + many
+    shapes = [t.shape for t in terms]
+    own_rows, columns = width // 32, 10 * HEAD_DIM
+    return pl.pallas_call(
+        functools.partial(attend_back_kernel, many),
+        out_shape=[
+            jax.ShapeDtypeStruct((tokens, width), bf16),
+            jax.ShapeDtypeStruct((own_rows, 3 * width), f32),
+            jax.ShapeDtypeStruct((4, 1, own_rows), f32),
+            jax.ShapeDtypeStruct((1, 3), f32),
+        ]
+        + [jax.ShapeDtypeStruct((r // 32, c), f32) for r, c in shapes],
+        in_specs=[vmem] * 7 + [smem] + [vmem] * (5 + many),
+        out_specs=[vmem] * (4 + many),
+        scratch_shapes=[pltpu.VMEM((r, c // 2), bf16) for r, c in shapes]
+        + [pltpu.VMEM((6, r // 8, c // 2), bf16) for r, c in shapes]
+        + [pltpu.VMEM((r // 4, c // 2), bf16) for r, c in shapes]
+        + [pltpu.VMEM((3, r // 16, c // 2), bf16) for r, c in shapes]
+        + [pltpu.VMEM((r // 16, c // 2), f32) for r, c in shapes]
+        + [
+            pltpu.VMEM((3, 4) + block, bf16),
+            pltpu.VMEM((3, 4, 2 * tokens, HEAD_DIM), bf16),
+            pltpu.VMEM((3, 4, 2 * tokens, HEAD_DIM), bf16),
+            pltpu.VMEM((4,) + block, bf16),
+            pltpu.VMEM((4, 1, tokens), f32),
+            pltpu.VMEM((3, 4, 2, 2) + block, f32),
+            pltpu.VMEM((3, 4, 2) + block, bf16),
+            pltpu.VMEM((3, 4, 2) + block, bf16),
+            pltpu.VMEM((4, 10) + block, bf16),
+            pltpu.VMEM((3, HEADS) + block, bf16),
+            pltpu.VMEM((16, 2, own_rows, columns), f32),
+            pltpu.VMEM((16, own_rows, columns), f32),
+            pltpu.VMEM((16 * own_rows, columns), bf16),
+            pltpu.VMEM((6, 2 * own_rows, columns), bf16),
+            pltpu.VMEM((4, own_rows, columns), f32),
+            pltpu.VMEM((4, own_rows, columns), f32),
+            pltpu.VMEM((tokens, width), f32),
+            pltpu.VMEM((2,) + small.shape, f32),
+            pltpu.VMEM((4,) + small.shape, f32),
+            pltpu.VMEM((4,) + small.shape, f32),
+            pltpu.SemaphoreType.DMA((copies,)),
+            pltpu.SemaphoreType.DMA((copies,)),
+        ],
+        compiler_params=pltpu.CompilerParams(
+            collective_id=2, has_side_effects=True, vmem_limit_bytes=62 * 2**20
+        ),
+    )(gmix, *saved, span, block_input, gain, w_qkv, grad_middle, small, *terms)
+
+
+def per_device_planned(
+    block_input,
+    out_grad,
+    seq_span,
+    ln1_gain,
+    ln1_bias,
+    w_qkv,
+    w_out,
+    ln2_gain,
+    ln2_bias,
+    w_up,
+    w_down,
+):
+    tokens, width = block_input.shape
+    mixed, *saved = attend(block_input, ln1_gain, ln1_bias, w_qkv, seq_span)
+    mixed = mixed.reshape(width, tokens)
+    block_output, grad_middle, grad_mixed, *terms, small = middle_part(
+        mixed, block_input, out_grad, w_out, w_up, w_down, ln2_gain, ln2_bias, seq_span
+    )
+    input_grad, sum_qkv, vecs, rms_stats, sum_down, sum_up, sum_out = attend_back(
+        grad_mixed.reshape(HEADS, HEAD_DIM, tokens),
+        saved,
+        seq_span,
+        block_input,
+        ln1_gain,
+        w_qkv,
+        grad_middle,
+        small,
+        terms,
+    )
+    vecs = vecs.reshape(4, -1)
+    return (
+        block_output,
+        input_grad,
+        vecs[0],
+        vecs[1],
+        sum_qkv,
+        sum_out,
+        vecs[2],
+        vecs[3],
+        sum_up,
+        sum_down,
+        rms_stats.reshape(3),
+    )
+
+
 def solution(mesh):
     placed = (
         P(("grp", "seq"), None),
@@ -286,8 +1176,9 @@
         P(),
         P(),
     )
+    planned = mesh.shape["grp"] == 4 and mesh.shape["seq"] == 8
     return jax.shard_map(
-        per_device,
+        per_device_planned if planned else per_device,
         mesh=mesh,
         in_specs=placed,
         out_specs=(

time: 912 us -> 182 us (0.20)
  waiting for transfers between devices: 534 us -> 0 us
  Pallas kernels: 0 us -> 160 us
  starting transfers between devices: 139 us -> 0 us
  matrix products: 60.1 us -> 0 us
  blocking collectives: 42 us -> 0 us
  other arithmetic: 39.7 us -> 0 us
  local copies, waits for them, and re-layouts: 59.9 us -> 20.5 us
  between operations: 16 us -> 0.71 us
  loops' own time: 10.8 us -> 0 us
    reduce_scatter x4 -> x0, waiting for transfers between devices: 331 us -> none  [the longest x1 142 us: per_device(): lax.psum_scatter(grad_w_down, ('grp', 'seq'), scatter_dimension=0, tiled=...]
    ppermute x22 -> x0, waiting for transfers between devices: 203 us -> none  [the longest x8 196 us: shifted(): lax.ppermute(array, axis, [(i, (i + by) % devices) for i in range(devices)])]
    pallas_call x0 -> x3, Pallas kernels: none -> 160 us  [the longest x1 93.6 us: attend_back(): pl.pallas_call(functools.partial(attend_back_kernel, many), out_shape=[ja...]
    ppermute x22 -> x0, starting transfers between devices: 139 us -> none  [the longest x14 134 us: passed_along(): return lax.ppermute(array, axis, pairs)]
    dot_general x19 -> x0, matrix products: 60.1 us -> none  [the longest x4 21.9 us: contract_rows(): lax.dot_general(left, right, (((0,), (0,)), ((), ())), preferred_element_...]
    unnamed x1 -> x0, blocking collectives: 42 us -> none
    while x14 -> x0, local copies, waits for them, and re-layouts: 28.9 us -> none
    add x10 -> x0, other arithmetic: 16 us -> none  [the longest x7 16 us: backward_hop(): return (moving, grad_acc + new_terms, grad_run)]
  transfers between devices with their start and end apart: 26 -> 0, of which waited for: 22 -> 0; matrix products, arithmetic and copies ran while one was open for 10% -> 0% of each run, Pallas kernels for 0% -> 0%
where the time goes in v3:
time: 182 us; the launch traced here: 181 us
  Pallas kernels  160 us (88%)
  local copies, waits for them, and re-layouts  20.5 us (11%)
    pallas_call x1, Pallas kernels, attend_back(): pl.pallas_call(functools.partial(attend_back_kernel, many), out_shape=[ja...  93.6 us
    pallas_call x1, Pallas kernels, attend(): pl.pallas_call(attend_kernel, out_shape=[jax.ShapeDtypeStruct((HEADS,) +...  47.6 us
    unnamed x40, local copies, waits for them, and re-layouts  19.3 us
    pallas_call x1, Pallas kernels, middle_part(): pl.pallas_call(functools.partial(middle_kernel, 512), out_shape=[jax.Shap...  18.4 us

profile of v3, /device:TPU:0, one launch (start us, length us, event | category | flops | bytes accessed | tf_op | source)
XLA Modules:
  0.0 180.8 jit_solution(7049166558187963636)
XLA Ops:
  0.6 0.0 copy-start
  0.7 1.0 copy-done
  1.6 0.0 copy-start.11
  1.6 0.7 copy-done.11
  2.3 0.0 copy-start.13
  2.3 0.7 copy-done.13
  3.0 0.0 copy-start.16
  3.0 0.7 copy-done.16
  3.7 0.0 copy-start.2
  3.7 0.0 copy-start.7
  3.7 0.0 copy-start.14
  3.7 0.0 copy-start.15
  3.7 47.6 %shard_map.194 = (bf16[12,64,256]{2,1,0:T(8,128)(2,1)S(1)}, bf16[3,4,64,256]{3,2,1,0:T(8,128)(2,1)S(1)}, bf16[3,4,2,2,64,256]{5,4,3,2,1,0:T(8,128)(2,1)S(1)}, bf...) custom-call(bf16[256,768]{1,0:T(8,128)(2,1)S(1)} %copy-done, ...), custom_call_target="tpu_custom_call" | custom-call | tf_op jit(solution)/shard_map/pallas_call | solution.py:544
  51.3 0.0 copy-start.1
  51.3 1.2 copy-done.1
  52.5 0.0 copy-start.3
  52.5 1.1 copy-done.3
  53.6 0.0 copy-start.8
  53.6 0.7 copy-done.8
  54.3 0.0 copy-start.12
  54.3 0.6 copy-done.12
  54.9 0.0 copy-start.5
  54.9 0.0 copy-done.2
  54.9 0.0 copy-done.7
  54.9 0.0 copy-done.14
  54.9 0.0 copy-done.15
  54.9 18.4 %shard_map.195 = (bf16[256,768]{1,0:T(8,128)(2,1)}, f32[256,768]{1,0:T(8,128)S(1)}, bf16[768,256]{1,0:T(8,128)(2,1)S(1)}, bf16[3072,768]{1,0:T(8,128)(2,1)}, bf1...) custom-call(bf16[768,256]{1,0:T(8,128)(2,1)S(1)} %bitcast.11, ...), custom_call_target="tpu_custom_call" | custom-call | tf_op jit(solution)/shard_map/pallas_call | solution.py:658
  73.3 0.0 copy-done.5
  73.3 0.0 copy-start.4
  73.3 1.0 copy-done.4
  74.3 0.0 copy-start.6
  74.3 0.9 copy-done.6
  75.2 0.0 copy-start.9
  75.2 0.7 copy-done.9
  76.0 0.0 copy-start.10
  76.0 0.6 copy-done.10
  76.6 93.6 %shard_map.196 = (bf16[256,768]{1,0:T(8,128)(2,1)}, f32[24,2304]{1,0:T(8,128)}, f32[4,1,24]{2,1,0:T(1,128)}, f32[1,3]{1,0:T(1,128)}, f32[96,768]{1,0:T(8,128)}, /*index=5*/f32[24,3072]{1,0:T(8,128)}, f32[24,768]{1,0:T(8,128)}) custom-call(bf16[12,64,256]{2,1,0:T(8,128)(2,1)} %bitcast.12, bf16[3,4,64,256]{3,2,1,0:T(8,128)(2,1)} %copy-done.8, ...), custom_call_target="tpu_custom_call" | custom-call | tf_op jit(solution)/shard_map/pallas_call | solution.py:1073
  170.2 1.2 slice_bitcast_fusion
  171.4 1.8 copy.28
  173.2 1.6 copy.29
  174.8 1.5 copy.30
  176.3 1.7 copy.31
  178.0 1.7 copy.32
  179.7 1.1 copy.33
Async XLA Ops:
  0.6 1.0 copy-start
  1.6 0.7 copy-start.11
  2.3 0.7 copy-start.13
  3.0 0.7 copy-start.16
  3.7 51.2 %copy-start.2 = (bf16[768,768]{1,0:T(8,128)(2,1)S(1)}, bf16[768,768]{1,0:T(8,128)(2,1)}, u32[]{:S(2)}) copy-start(bf16[768,768]{1,0:T(8,128)(2,1)} %w_out.1) | copy-start | bytes 3538948
  3.7 51.2 %copy-start.7 = (bf16[256,768]{1,0:T(8,128)(2,1)S(1)}, bf16[256,768]{1,0:T(8,128)(2,1)}, u32[]{:S(2)}) copy-start(bf16[256,768]{1,0:T(8,128)(2,1)} %out_grad.1) | copy-start | bytes 1179652
  3.7 51.2 %copy-start.14 = (f32[768]{0:T(1024)S(1)}, f32[768]{0:T(1024)}, u32[]{:S(2)}) copy-start(f32[768]{0:T(1024)} %gain.3) | copy-start | bytes 9220
  3.7 51.2 %copy-start.15 = (f32[768]{0:T(1024)S(1)}, f32[768]{0:T(1024)}, u32[]{:S(2)}) copy-start(f32[768]{0:T(1024)} %bias.3) | copy-start | bytes 9220
  51.3 1.2 copy-start.1
  52.5 1.1 copy-start.3
  53.6 0.7 copy-start.8
  54.3 0.6 copy-start.12
  54.9 18.4 %copy-start.5 = (f32[3,4,64,256]{3,2,1,0:T(8,128)}, f32[3,4,64,256]{3,2,1,0:T(8,128)S(1)}, u32[]{:S(2)}) copy-start(f32[3,4,64,256]{3,2,1,0:T(8,128)S(1)} %get-tuple-element.38.refs_4_) | copy-start | bytes 2359300
  73.3 1.0 copy-start.4
  74.3 0.9 copy-start.6
  75.2 0.7 copy-start.9
  76.0 0.6 copy-start.10
